TPU v7x, 32 devices: a whole 2x2x4 slice. The times are simulated.
32 devices in a mesh: row: 8 (over z, x), col: 2 (over core), grp: 2 (over y).
Axes of the slice: x: 2, y: 2, z: 4, core: 2. Of those that a mesh axis runs over, the one named last changes fastest.
Arguments:
- patches: bfloat16 [2, 512, 1408], P('grp', 'row', 'col'), may hold values from -6 to 6
- vis_gain: bfloat16 [1408], P('col'), may hold values from 0.25 to 1.75
- vis_bias: bfloat16 [1408], P('col'), may hold values from -3 to 3
- vis_qkv: bfloat16 [1408, 4224], P('col', 'row'), may hold values from -1 to 1
- vis_qkv_bias: bfloat16 [4224], P('row'), may hold values from -3 to 3
- vis_out: bfloat16 [1408, 1408], P('row', 'col'), may hold values from -0.15625 to 0.15625
- vis_out_bias: bfloat16 [1408], P('col'), may hold values from -3 to 3
- proj_weight: bfloat16 [4, 1408, 1408], P(None, 'col', 'row'), may hold values from -0.078125 to 0.078125
- proj_bias: bfloat16 [1408], P('row'), may hold values from -3 to 3
- text_embeds: bfloat16 [2, 2048, 1408], P('grp', 'col', 'row'), may hold values from -6 to 6
- dec_gain: bfloat16 [1408], P('row'), may hold values from 0.25 to 1.75
- dec_qkv: bfloat16 [1408, 4224], P('row', 'col'), may hold values from -1 to 1
- dec_out: bfloat16 [1408, 1408], P('col', 'row'), may hold values from -0.15625 to 0.15625
- image_tokens: int32 [2, 8], P('grp'), may hold values from 1 to 32, 128 in all within a row
- text_gaps: int32 [2, 9], P('grp'), may hold values from 1 to 960, 1920 in all within a row
- doc_lengths: int32 [4], replicated, may hold values from 1 to 2048, 4096 in all
Outputs:
- hidden_out: bfloat16 [2, 2048, 1408], P('grp', 'col', 'row')
All inputs are finite; a program needn't handle non-finite values.
Results may differ from a plain program's by a relative error of at most 0.0045.
The roundings to bfloat16 on the way count: a program that leaves them out, or rounds other values in their place, can miss the bound.
Values may be sent and summed in bfloat16 or wider, within the bound.
A program may use at most 64 MiB of HBM per device.

v0:
```python
import math

import jax
import jax.numpy as jnp
from jax import lax
from jax.sharding import PartitionSpec as P

HEADS = 16
HEAD_DIM = 88


def rows_over_col(values):
    return lax.all_gather(values, "col", axis=0, tiled=True)


def rows_over_row(values):
    return lax.all_gather(values, "row", axis=0, tiled=True)


def sums_over_col(term_fn, count):
    return lax.psum_scatter(
        term_fn(jnp.int32(0), lax.axis_size("col") * count), "col", scatter_dimension=0, tiled=True
    )


def segment_of(index_values, lengths):
    ends = jnp.cumsum(lengths, dtype=jnp.int32)
    return jnp.sum(
        (index_values[:, None] >= ends[None, :]).astype(jnp.int32), axis=1, dtype=jnp.int32
    )


def insert_map(text_rows, image_lengths, gaps):
    offsets = jnp.cumsum(image_lengths, dtype=jnp.int32) - image_lengths
    starts = jnp.cumsum(gaps, dtype=jnp.int32)[: image_lengths.shape[0]] + offsets
    inside = (text_rows[:, None] >= starts[None, :]) & (
        text_rows[:, None] < (starts + image_lengths)[None, :]
    )
    source = jnp.sum(
        jnp.where(inside, offsets[None, :] + text_rows[:, None] - starts[None, :], 0),
        axis=1,
        dtype=jnp.int32,
    )
    return (source, jnp.any(inside, axis=1))


def product_rows(left, right):

    def term(start, count):
        return jnp.dot(left, right, preferred_element_type=jnp.float32)

    return term


def empty_state(heads, rows):
    return (
        jnp.full((heads, rows), -1e30, jnp.float32),
        jnp.zeros((heads, rows), jnp.float32),
        jnp.zeros((rows, heads, HEAD_DIM), jnp.float32),
    )


def online_block(carry, query, keys, values, usable, scale):
    best, norm_sum, accum = carry
    piece_scores = (
        jnp.einsum("qhe,khe->hqk", query, keys, preferred_element_type=jnp.float32) * scale
    )
    piece_scores = jnp.where(usable, piece_scores, -1e30)
    new_best = jnp.maximum(best, jnp.max(piece_scores, axis=2))
    piece_weights = jnp.where(usable, jnp.exp(piece_scores - new_best[:, :, None]), 0.0)
    factor = jnp.exp(best - new_best)
    norm_sum = norm_sum * factor + jnp.sum(piece_weights, axis=2)
    added = jnp.einsum(
        "hqk,khe->qhe",
        piece_weights.astype(jnp.bfloat16),
        values,
        preferred_element_type=jnp.float32,
    )
    accum = accum * jnp.transpose(factor)[:, :, None] + added
    return (new_best, norm_sum, accum)


def fold_keys(carry, query, keyval, key_marks, mask_of, scale):
    count = keyval.shape[0]
    heads = query.shape[1]
    block = math.gcd(count, 512)
    blocks = count // block
    shaped = keyval.reshape(blocks, block, heads, 2, HEAD_DIM)
    marks = key_marks.reshape(blocks, block)

    def advance(state, inputs):
        piece, piece_marks = inputs
        return (
            online_block(state, query, piece[:, :, 0], piece[:, :, 1], mask_of(piece_marks), scale),
            None,
        )

    carry, unused = lax.scan(advance, carry, (shaped, marks))
    return carry


def per_device(
    patches,
    vis_gain,
    vis_bias,
    vis_qkv,
    vis_qkv_bias,
    vis_out,
    vis_out_bias,
    proj_weight,
    proj_bias,
    text_embeds,
    dec_gain,
    dec_qkv,
    dec_out,
    image_tokens,
    text_gaps,
    doc_lengths,
):
    width = HEADS * HEAD_DIM
    scale = HEAD_DIM ** (-0.5)
    col_count = lax.axis_size("col")
    row_count = lax.axis_size("row")
    image_lengths = image_tokens[0]
    gaps = text_gaps[0]
    xfull = patches[0].astype(jnp.float32)
    rows_b = xfull.shape[0]
    sum_one, sum_two = lax.psum((jnp.sum(xfull, axis=1), jnp.sum(xfull * xfull, axis=1)), "col")
    mean = sum_one[:, None] / width
    variance = sum_two[:, None] / width - mean * mean
    normed = (
        (xfull - mean) * lax.rsqrt(variance + 1e-06) * vis_gain.astype(jnp.float32)
        + vis_bias.astype(jnp.float32)
    ).astype(jnp.bfloat16)
    gathered = rows_over_row(normed)
    patch_total = gathered.shape[0]
    rows_a = patch_total // col_count
    qkv_rows = (
        sums_over_col(product_rows(gathered, vis_qkv), rows_a) + vis_qkv_bias.astype(jnp.float32)
    ).astype(jnp.bfloat16)
    heads_row = qkv_rows.shape[1] // (3 * HEAD_DIM)
    qkv_rows = qkv_rows.reshape(rows_a, heads_row, 3, HEAD_DIM)
    query = qkv_rows[:, :, 0]
    keyval = qkv_rows[:, :, 1:].reshape(rows_a, heads_row * 2 * HEAD_DIM)
    all_keyval = rows_over_col(keyval)
    first_row = lax.axis_index("col") * rows_a
    query_ids = segment_of((first_row + jnp.arange(rows_a, dtype=jnp.int32)) // 4, image_lengths)
    key_ids = segment_of(jnp.arange(patch_total, dtype=jnp.int32) // 4, image_lengths)

    def same_image(marks):
        return (query_ids[:, None] == marks[None, :])[None]

    best_vis, norm_vis, accum_vis = fold_keys(
        empty_state(heads_row, rows_a), query, all_keyval, key_ids, same_image, scale
    )
    vis_attn = (
        (accum_vis / jnp.transpose(norm_vis)[:, :, None])
        .astype(jnp.bfloat16)
        .reshape(rows_a, heads_row * HEAD_DIM)
    )
    all_attn = rows_over_col(vis_attn)
    delta = lax.psum_scatter(
        product_rows(all_attn, vis_out)(jnp.int32(0), lax.axis_size("row") * rows_b),
        "row",
        scatter_dimension=0,
        tiled=True,
    )
    resid = (xfull + delta + vis_out_bias.astype(jnp.float32)).astype(jnp.bfloat16)
    merged = resid.reshape(rows_b // 4, 4 * resid.shape[1])
    all_merged = rows_over_row(merged)
    partial_value = jnp.dot(
        all_merged,
        proj_weight.reshape(4 * proj_weight.shape[1], proj_weight.shape[2]),
        preferred_element_type=jnp.float32,
    )
    text = text_embeds[0]
    rows_text_a = text.shape[0]
    text_total = rows_text_a * col_count

    def place_term(start, count):
        source, inside = insert_map(jnp.arange(count, dtype=jnp.int32), image_lengths, gaps)
        return jnp.where(inside[:, None], jnp.take(partial_value, source, axis=0), 0.0)

    placed = sums_over_col(place_term, rows_text_a)
    own_rows = lax.axis_index("col") * rows_text_a + jnp.arange(rows_text_a, dtype=jnp.int32)
    unused, own_inside = insert_map(own_rows, image_lengths, gaps)
    dec_input = jnp.where(
        own_inside[:, None], placed + proj_bias.astype(jnp.float32), text.astype(jnp.float32)
    ).astype(jnp.bfloat16)
    xdec = dec_input.astype(jnp.float32)
    squares = lax.psum(jnp.sum(xdec * xdec, axis=1), "row")
    dec_normed = (
        xdec * lax.rsqrt(squares[:, None] / width + 1e-05) * dec_gain.astype(jnp.float32)
    ).astype(jnp.bfloat16)
    rows_text_b = text_total // row_count
    gathered_text = rows_over_col(dec_normed)
    dec_rows = lax.psum_scatter(
        product_rows(gathered_text, dec_qkv)(jnp.int32(0), lax.axis_size("row") * rows_text_b),
        "row",
        scatter_dimension=0,
        tiled=True,
    ).astype(jnp.bfloat16)
    heads_col = dec_rows.shape[1] // (3 * HEAD_DIM)
    dec_rows = dec_rows.reshape(rows_text_b, heads_col, 3, HEAD_DIM)
    dec_query = dec_rows[:, :, 0]
    dec_keyval = dec_rows[:, :, 1:].reshape(rows_text_b, heads_col * 2 * HEAD_DIM)
    half = lax.axis_index("grp")
    in_half = lax.axis_index("row") * rows_text_b + jnp.arange(rows_text_b, dtype=jnp.int32)
    query_pos = (
        in_half // rows_text_b * (2 * rows_text_b) + half * rows_text_b + in_half % rows_text_b
    )
    query_doc = segment_of(query_pos, doc_lengths)

    def causal_doc(key_pos):
        key_doc = segment_of(key_pos, doc_lengths)
        return (
            (key_doc[None, :] == query_doc[:, None]) & (key_pos[None, :] <= query_pos[:, None])
        )[None]

    start_state = empty_state(heads_col, rows_text_b)
    piece = lax.all_gather(dec_keyval, ("row", "grp"), axis=0, tiled=True)
    key_pos = jnp.arange(piece.shape[0], dtype=jnp.int32)
    best, norm_sum, accum = fold_keys(start_state, dec_query, piece, key_pos, causal_doc, scale)
    dec_attn = (
        (accum / jnp.transpose(norm_sum)[:, :, None])
        .astype(jnp.bfloat16)
        .reshape(rows_text_b, heads_col * HEAD_DIM)
    )
    all_dec_attn = rows_over_row(dec_attn)
    dec_delta = sums_over_col(product_rows(all_dec_attn, dec_out), rows_text_a)
    return (xdec + dec_delta).astype(jnp.bfloat16)[None]


def solution(mesh):
    return jax.shard_map(
        per_device,
        mesh=mesh,
        in_specs=(
            P("grp", "row", "col"),
            P("col"),
            P("col"),
            P("col", "row"),
            P("row"),
            P("row", "col"),
            P("col"),
            P(None, "col", "row"),
            P("row"),
            P("grp", "col", "row"),
            P("row"),
            P("row", "col"),
            P("col", "row"),
            P("grp", None),
            P("grp", None),
            P(),
        ),
        out_specs=P("grp", "col", "row"),
        check_vma=False,
    )
```

profile of v0, /device:TPU:0, one launch (start us, length us, event | category | flops | bytes accessed | tf_op | source)
XLA Modules:
  0.0 856.6 jit_solution(4732098955174306663)
XLA Ops:
  10.0 2.6 all-reduce
  13.6 33.9 %all_gather.21 = bf16[512,704]{1,0:T(8,128)(2,1)S(1)} all-gather(bf16[64,704]{1,0:T(8,128)(2,1)S(1)} %fusion.43), channel_id=1, replica_groups=mesh['row'=8,'col'=2,'grp'=2] {'row'}, dimensions={0}, use_global_device_ids=true | all-gather | bytes 811008 | tf_op jit(solution)/shard_map/all_gather | solution.py:17
  47.5 1.6 fusion.58
  49.8 8.9 %reduce-scatter.6.cloned.1.call-done = f32[256,528]{0,1:T(8,128)} async-done(((f32[512,528]{0,1:T(8,128)}), f32[256,528]{0,1:T(8,128)}) %reduce-scatter.6.cloned.1.call-update) | async-done | bytes 540688 | tf_op jit(solution)/shard_map/reduce_scatter | solution.py:21
  59.9 2.2 all_gather.22
  63.5 1.9 all_gather.23
  65.4 1.6 fusion.59
  67.1 1.8 copy.35
  70.3 62.9 %reduce-scatter.8.cloned.1.call-done = f32[64,704]{1,0:T(8,128)} async-done(((f32[512,704]{1,0:T(8,128)}), f32[64,704]{1,0:T(8,128)}) %reduce-scatter.8.cloned.1.call-update) | async-done | bytes 180240 | tf_op jit(solution)/shard_map/reduce_scatter | solution.py:162
  134.3 31.9 %all_gather.24 = bf16[128,2816]{1,0:T(8,128)(2,1)S(1)} all-gather(bf16[16,2816]{1,0:T(8,128)(2,1)S(1)} %reshape.283), channel_id=1, replica_groups=mesh['row'=8,'col'=2,'grp'=2] {'row'}, dimensions={0}, use_global_device_ids=true | all-gather | bytes 811008 | tf_op jit(solution)/shard_map/all_gather | solution.py:17
  166.7 6.6 gather_fusion
  173.3 1.7 copy.37
  175.0 2.7 select_select_fusion
  178.0 7.9 reduce-scatter.10.cloned.1.call-done
  187.1 21.6 %psum.23 = f32[1024]{0:T(1024)S(1)} all-reduce(f32[1024]{0:T(1024)S(1)} %get-tuple-element.236), channel_id=1, replica_groups=mesh['row'=8,'col'=2,'grp'=2] {'row'}, use_global_device_ids=true, to_apply=%region_17.18 | all-reduce | flops 1024 | bytes 8192 | tf_op jit(solution)/shard_map/psum | solution.py:191
  208.9 2.3 all_gather.25
  211.2 8.4 fusion.61
  219.7 290.6 %reduce-scatter.12.cloned.1.call-done = f32[256,2112]{0,1:T(8,128)} async-done(((f32[2048,2112]{0,1:T(8,128)}), f32[256,2112]{0,1:T(8,128)}) %reduce-scatter.12.cloned.1.call-update) | async-done | bytes 2162704 | tf_op jit(solution)/shard_map/reduce_scatter | solution.py:197
  510.4 1.7 convert_element_type.104
  513.6 171.5 %all-gather.3.cloned.1.call-done = bf16[4096,1408]{0,1:T(8,128)(2,1)} async-done(((bf16[256,1408]{0,1:T(8,128)(2,1)}), bf16[4096,1408]{0,1:T(8,128)(2,1)}) %all-gather.3.cloned.1.call-update) | async-done | bytes 11534352 | tf_op jit(solution)/shard_map/all_gather | solution.py:221
  685.1 7.7 copy.46
  692.9 9.1 %copy.39 = bf16[8,512,8,2,88]{1,4,2,3,0:T(8,128)(2,1)} copy(bf16[8,512,8,2,88]{1,0,4,3,2:T(8,128)(2,1)S(1)} %bitcast.175) | data formatting | bytes 23068672
  702.0 75.6 %while.5 = (s32[]{:T(128)}, f32[8,256]{1,0:T(8,128)S(1)}, f32[8,256]{1,0:T(8,128)S(1)}, f32[256,8,88]{0,2,1:T(8,128)S(1)}, s32[8,512]{1,0:T(8,128)S(1)}, /*index...) while((s32[]{:T(128)}, f32[8,256]{1,0:T(8,128)S(1)}, ...), condition=%wide.region_25.26_spmd.clone, body=%wide.region_21.25_spmd.clone.sunk | while | flops 383687936 | bytes 36158660 | solution.py:98
  702.3 1.5 dynamic-slice_bitcast_fusion.2
  703.8 2.9 fusion.85
  706.7 3.6 fusion.89
  711.8 1.5 dynamic-slice_bitcast_fusion.2
  713.2 2.9 fusion.85
  716.2 3.6 fusion.89
  721.2 1.5 dynamic-slice_bitcast_fusion.2
  722.7 2.9 fusion.85
  725.6 3.6 fusion.89
  730.7 1.5 dynamic-slice_bitcast_fusion.2
  732.1 2.9 fusion.85
  735.1 3.6 fusion.89
  740.1 1.5 dynamic-slice_bitcast_fusion.2
  741.6 2.9 fusion.85
  744.5 3.6 fusion.89
  751.0 2.9 fusion.85
  754.0 3.6 fusion.89
  760.5 2.9 fusion.85
  763.4 3.6 fusion.89
  769.9 2.9 fusion.85
  772.9 3.6 fusion.89
  778.5 58.3 %all-gather.5.cloned.1.call-done = bf16[2048,704]{0,1:T(8,128)(2,1)} async-done(((bf16[256,704]{0,1:T(8,128)(2,1)}), bf16[2048,704]{0,1:T(8,128)(2,1)}) %all-gather.5.cloned.1.call-update) | async-done | bytes 2883600 | tf_op jit(solution)/shard_map/all_gather | solution.py:17
  836.8 3.8 fusion.62
  840.5 7.3 reduce-scatter.14.cloned.1.call-done
  847.8 1.9 fusion.36
  (172 shorter events, 29.8 us)
Async XLA Ops:
  6.5 41.0 %copy-start = (bf16[704,528]{0,1:T(8,128)(2,1)S(1)}, bf16[704,528]{0,1:T(8,128)(2,1)}, u32[]{:S(2)}) copy-start(bf16[704,528]{0,1:T(8,128)(2,1)} %param.21) | copy-start | bytes 2230276
  6.5 42.7 %copy-start.7 = (bf16[528]{0:T(1024)(128)(2,1)S(1)}, bf16[528]{0:T(1024)(128)(2,1)}, u32[]{:S(2)}) copy-start(bf16[528]{0:T(1024)(128)(2,1)} %param.22) | copy-start | bytes 3172
  6.5 42.7 %copy-start.9 = (s32[1,8]{1,0:T(1,128)S(1)}, s32[1,8]{1,0:T(1,128)}, u32[]{:S(2)}) copy-start(s32[1,8]{1,0:T(1,128)} %param.31) | copy-start | bytes 100
  6.5 52.1 %reduce-scatter.6.cloned.1.call-start = ((), (), s32[]{:S(2)}) async-start(), calls=%async_computation.5 | async-start | bytes 1622016 | tf_op jit(solution)/shard_map/reduce_scatter | solution.py:21
  49.2 84.0 %reduce-scatter.8.cloned.1.call-start = ((), (), s32[]{:S(2)}) async-start(), calls=%async_computation.6 | async-start | bytes 1769472 | tf_op jit(solution)/shard_map/reduce_scatter | solution.py:162
  59.9 5.5 copy-start.6
  63.0 4.0 copy-start.8
  67.0 2.8 copy-start.10
  67.0 66.2 %copy-start.3 = (bf16[1,64,704]{2,1,0:T(8,128)(2,1)S(1)}, bf16[1,64,704]{2,1,0:T(8,128)(2,1)}, u32[]{:S(2)}) copy-start(bf16[1,64,704]{2,1,0:T(8,128)(2,1)} %param.18) | copy-start | bytes 270340
  67.0 118.8 %reduce-scatter.10.cloned.1.call-start = ((), (), s32[]{:S(2)}) async-start(), calls=%async_computation.7 | async-start | bytes 2162688 | tf_op jit(solution)/shard_map/reduce_scatter | solution.py:21
  175.0 2.8 copy-start.11
  175.0 2.8 copy-start.12
  175.0 10.8 %copy-start.5 = (bf16[1,1024,176]{1,2,0:T(8,128)(2,1)S(1)}, bf16[1,1024,176]{1,2,0:T(8,128)(2,1)}, u32[]{:S(2)}) copy-start(bf16[1,1024,176]{1,2,0:T(8,128)(2,1)} %param.27) | copy-start | bytes 1081348
  177.7 33.5 %copy-start.4 = (bf16[176,2112]{1,0:T(8,128)(2,1)S(1)}, bf16[176,2112]{1,0:T(8,128)(2,1)}, u32[]{:S(2)}) copy-start(bf16[176,2112]{1,0:T(8,128)(2,1)} %param.29) | copy-start | bytes 2230276
  177.8 332.6 %reduce-scatter.12.cloned.1.call-start = ((), (), s32[]{:S(2)}) async-start(), calls=%async_computation.8 | async-start | bytes 19464192 | tf_op jit(solution)/shard_map/reduce_scatter | solution.py:197
  219.7 293.6 %copy-start.13 = (s32[4]{0:T(128)S(1)}, s32[4]{0:T(128)}, u32[]{:S(2)}) copy-start(s32[4]{0:T(128)} %param.33) | copy-start | bytes 52
  219.7 465.4 %all-gather.3.cloned.1.call-start = ((), (), s32[]{:S(2)}) async-start(), calls=%async_computation.9 | async-start | bytes 12255232 | tf_op jit(solution)/shard_map/all_gather | solution.py:221
  513.0 323.7 %all-gather.5.cloned.1.call-start = ((), (), s32[]{:S(2)}) async-start(), calls=%async_computation.10 | async-start | bytes 3244032 | tf_op jit(solution)/shard_map/all_gather | solution.py:17
  706.7 3.6 copy-start.2
  716.2 3.6 copy-start.2
  725.6 3.6 copy-start.2
  735.1 3.6 copy-start.2
  744.5 3.6 copy-start.2
  754.0 3.6 copy-start.2
  763.4 3.6 copy-start.2
  772.9 3.6 copy-start.2
  778.4 71.4 %copy-start.1 = (bf16[704,528]{0,1:T(8,128)(2,1)S(1)}, bf16[704,528]{0,1:T(8,128)(2,1)}, u32[]{:S(2)}) copy-start(bf16[704,528]{0,1:T(8,128)(2,1)} %param.21) | copy-start | bytes 2230276
  778.4 69.4 %reduce-scatter.14.cloned.1.call-start = ((), (), s32[]{:S(2)}) async-start(), calls=%async_computation.11 | async-start | bytes 2162688 | tf_op jit(solution)/shard_map/reduce_scatter | solution.py:21
Sparse Core Ops, SparseCore 0:
  49.3 9.3 reduce-scatter.5
  67.1 66.0 reduce-scatter.7
  177.9 7.8 reduce-scatter.9
  219.8 290.5 reduce-scatter.11
  513.3 171.7 all-gather.2
  778.5 58.1 all-gather.4
  840.7 7.1 reduce-scatter.13
where the time goes:
time: 858 us; the launch traced here: 857 us
  waiting for transfers between devices  608 us (71%)
  blocking collectives  96.5 us (11%)
  matrix products  69.1 us (8%)
  local copies, waits for them, and re-layouts  40.9 us (5%)
  other arithmetic  27.7 us (3%)
  between operations  13.8 us (2%)
    reduce_scatter x1, waiting for transfers between devices, per_device(): lax.psum_scatter(product_rows(gathered_text, dec_qkv)(jnp.int32(0), lax.a...  291 us
    all_gather x1, waiting for transfers between devices, per_device(): piece = lax.all_gather(dec_keyval, ('row', 'grp'), axis=0, tiled=True)  171 us
    all_gather x2, blocking collectives, rows_over_row(): return lax.all_gather(values, 'row', axis=0, tiled=True)  65.8 us
    reduce_scatter x1, waiting for transfers between devices, per_device(): lax.psum_scatter(product_rows(all_attn, vis_out)(jnp.int32(0), lax.axis_s...  62.9 us
    all_gather x1, waiting for transfers between devices, rows_over_row(): return lax.all_gather(values, 'row', axis=0, tiled=True)  58.3 us
    dot_general x9, matrix products, online_block(): jnp.einsum('hqk,khe->qhe', piece_weights.astype(jnp.bfloat16), values, pr...  29.5 us
    reduce_scatter x3, waiting for transfers between devices, sums_over_col(): lax.psum_scatter(term_fn(jnp.int32(0), lax.axis_size('col') * count), 'co...  24 us
    dot_general x9, matrix products, online_block(): jnp.einsum('qhe,khe->hqk', query, keys, preferred_element_type=jnp.float32)  23.8 us
  transfers between devices with their start and end apart: 7, of which 7 were waited for; matrix products, arithmetic and copies ran while one was open for 0% of the time, Pallas kernels for 0%

commit v1 on v0

v1 whole, which is shorter than its diff:
```python
import functools

import jax
import jax.numpy as jnp
from jax import lax
from jax.experimental import pallas as pl
from jax.experimental.pallas import tpu as pltpu
from jax.sharding import PartitionSpec as P

HEADS = 16
HEAD_DIM = 88
PAD = 128
TPD = 256
LOG2E = 1.4426950408889634
F32 = jnp.float32
BF16 = jnp.bfloat16


def starts_of(index_values, lengths):
    ends = jnp.cumsum(lengths, dtype=jnp.int32)
    past = index_values[:, None] >= ends[None, :]
    return jnp.sum(jnp.where(past, lengths[None, :], 0), axis=1, dtype=jnp.int32)


def segment_of(index_values, lengths):
    ends = jnp.cumsum(lengths, dtype=jnp.int32)
    return jnp.sum((index_values[:, None] >= ends[None, :]).astype(jnp.int32), axis=1, dtype=jnp.int32)


def insert_map(text_rows, image_lengths, gaps):
    offsets = jnp.cumsum(image_lengths, dtype=jnp.int32) - image_lengths
    starts = jnp.cumsum(gaps, dtype=jnp.int32)[: image_lengths.shape[0]] + offsets
    inside = (text_rows[:, None] >= starts[None, :]) & (
        text_rows[:, None] < (starts + image_lengths)[None, :]
    )
    source = jnp.sum(
        jnp.where(inside, offsets[None, :] + text_rows[:, None] - starts[None, :], 0),
        axis=1,
        dtype=jnp.int32,
    )
    return (source, jnp.any(inside, axis=1))


def vis_head_kernel(
    x_ref, gain_ref, bias_ref, w_ref, wb_ref, ids_ref, idk_ref, o_ref, *, scale, width
):
    parts, count = x_ref.shape[0], x_ref.shape[1]
    one = jnp.zeros((count, 1), F32)
    two = jnp.zeros((count, 1), F32)
    for c in range(parts):
        x = x_ref[c].astype(F32)
        one += jnp.sum(x, axis=1, keepdims=True)
        two += jnp.sum(x * x, axis=1, keepdims=True)
    mean = one / width
    inv = lax.rsqrt(two / width - mean * mean + 1e-06)
    qkv = jnp.zeros((count, 3 * PAD), F32)
    for c in range(parts):
        x = x_ref[c].astype(F32)
        normed = ((x - mean) * inv * gain_ref[c].astype(F32) + bias_ref[c].astype(F32)).astype(BF16)
        qkv += jnp.dot(normed, w_ref[c], preferred_element_type=F32)
    qkv = (qkv + wb_ref[...].astype(F32)).astype(BF16)
    q, k, v = qkv[:, :PAD], qkv[:, PAD : 2 * PAD], qkv[:, 2 * PAD :]
    scores = lax.dot_general(q, k, (((1,), (1,)), ((), ())), preferred_element_type=F32)
    scores = scores * (scale * LOG2E)
    allowed = ids_ref[...] == idk_ref[...]
    scores = jnp.where(allowed, scores, -1e30)
    top = jnp.max(scores, axis=1, keepdims=True)
    weights = jnp.where(allowed, jnp.exp2(scores - top), 0.0)
    total = jnp.sum(weights, axis=1, keepdims=True)
    mixed = jnp.dot(weights.astype(BF16), v, preferred_element_type=F32) / total
    o_ref[...] = mixed.astype(BF16)


def vis_head(x, gain, bias, w, wb, ids, scale):
    count = x.shape[1]
    return pl.pallas_call(
        functools.partial(vis_head_kernel, scale=scale, width=HEADS * HEAD_DIM),
        out_shape=jax.ShapeDtypeStruct((count, PAD), BF16),
        compiler_params=pltpu.CompilerParams(vmem_limit_bytes=48 << 20),
        name="vis_head",
    )(x, gain, bias, w, wb, ids[:, None], ids[None, :])


def dec_qkv_kernel(x_ref, gain_ref, w_ref, o_ref, *, width):
    parts, count = x_ref.shape[1], x_ref.shape[2]
    squares = jnp.zeros((count, 1), F32)
    for r in range(parts):
        x = x_ref[0, r].astype(F32)
        squares += jnp.sum(x * x, axis=1, keepdims=True)
    inv = lax.rsqrt(squares / width + 1e-05)
    qkv = jnp.zeros((count, 3 * PAD), F32)
    for r in range(parts):
        x = x_ref[0, r].astype(F32)
        normed = (x * inv * gain_ref[r].astype(F32)).astype(BF16)
        qkv += jnp.dot(normed, w_ref[r], preferred_element_type=F32)
    o_ref[0] = qkv.astype(BF16)


def dec_rows(x, gain, w, tile):
    groups, parts, count, depth = x.shape
    return pl.pallas_call(
        functools.partial(dec_qkv_kernel, width=HEADS * HEAD_DIM),
        grid=(groups, count // tile),
        in_specs=[
            pl.BlockSpec((1, parts, tile, depth), lambda i, j: (i, 0, j, 0)),
            pl.BlockSpec(gain.shape, lambda i, j: (0, 0, 0)),
            pl.BlockSpec(w.shape, lambda i, j: (0, 0, 0)),
        ],
        out_specs=pl.BlockSpec((1, tile, 3 * PAD), lambda i, j: (i, j, 0)),
        out_shape=jax.ShapeDtypeStruct((groups, count, 3 * PAD), BF16),
        compiler_params=pltpu.CompilerParams(vmem_limit_bytes=48 << 20),
        name="dec_rows",
    )(x, gain, w)


def dec_attn_kernel(low_ref, q_ref, start_ref, pos_ref, k_ref, v_ref, o_ref, *, scale):
    b = pl.program_id(0)
    q = q_ref[...]
    begin = start_ref[...]
    at = pos_ref[...]
    count = q.shape[0]
    chunk = 2 * TPD

    def step(j, carry):
        best, norm, accum = carry
        rows = pl.ds(pl.multiple_of(j * TPD, TPD), TPD)
        k = jnp.concatenate([k_ref[0, rows], k_ref[1, rows]], axis=0)
        v = jnp.concatenate([v_ref[0, rows], v_ref[1, rows]], axis=0)
        scores = lax.dot_general(q, k, (((1,), (1,)), ((), ())), preferred_element_type=F32)
        scores = scores * (scale * LOG2E)
        key_at = j * chunk + lax.broadcasted_iota(jnp.int32, (count, chunk), 1)
        allowed = (key_at >= begin) & (key_at <= at)
        scores = jnp.where(allowed, scores, -1e30)
        new_best = jnp.maximum(best, jnp.max(scores, axis=1, keepdims=True))
        weights = jnp.where(allowed, jnp.exp2(scores - new_best), 0.0)
        factor = jnp.exp2(best - new_best)
        norm = norm * factor + jnp.sum(weights, axis=1, keepdims=True)
        accum = accum * factor + jnp.dot(weights.astype(BF16), v, preferred_element_type=F32)
        return new_best, norm, accum

    init = (
        jnp.full((count, 1), -1e30, F32),
        jnp.zeros((count, 1), F32),
        jnp.zeros((count, PAD), F32),
    )
    best, norm, accum = lax.fori_loop(low_ref[b], b + 1, step, init)
    o_ref[...] = (accum / norm).astype(BF16)


def dec_attn(q, k, v, begin, at, scale):
    count = q.shape[0]
    low = begin[::TPD] // (2 * TPD)
    return pl.pallas_call(
        functools.partial(dec_attn_kernel, scale=scale),
        grid_spec=pltpu.PrefetchScalarGridSpec(
            num_scalar_prefetch=1,
            grid=(count // TPD,),
            in_specs=[
                pl.BlockSpec((TPD, PAD), lambda i, s: (i, 0)),
                pl.BlockSpec((TPD, 1), lambda i, s: (i, 0)),
                pl.BlockSpec((TPD, 1), lambda i, s: (i, 0)),
                pl.BlockSpec(k.shape, lambda i, s: (0, 0, 0)),
                pl.BlockSpec(v.shape, lambda i, s: (0, 0, 0)),
            ],
            out_specs=pl.BlockSpec((TPD, PAD), lambda i, s: (i, 0)),
        ),
        out_shape=jax.ShapeDtypeStruct((count, PAD), BF16),
        compiler_params=pltpu.CompilerParams(vmem_limit_bytes=48 << 20),
        name="dec_attn",
    )(low, q, begin[:, None], at[:, None], k, v)


def pad_parts(w):
    lead = w.shape[:-1]
    w = w.reshape(lead + (3, HEAD_DIM))
    w = jnp.pad(w, [(0, 0)] * (len(lead) + 1) + [(0, PAD - HEAD_DIM)])
    return w.reshape(lead + (3 * PAD,))


def per_device(
    patches,
    vis_gain,
    vis_bias,
    vis_qkv,
    vis_qkv_bias,
    vis_out,
    vis_out_bias,
    proj_weight,
    proj_bias,
    text_embeds,
    dec_gain,
    dec_qkv,
    dec_out,
    image_tokens,
    text_gaps,
    doc_lengths,
):
    scale = HEAD_DIM ** (-0.5)
    C = lax.axis_size("col")
    R = lax.axis_size("row")
    c = lax.axis_index("col")
    r = lax.axis_index("row")
    g = lax.axis_index("grp")
    hr = HEADS // R
    hc = HEADS // C
    share = R // hc
    image_lengths = image_tokens[0]
    gaps = text_gaps[0]
    text = text_embeds[0]
    half_rows = text.shape[0] * C
    own_text = text.shape[0]

    x_all = lax.all_gather(patches[0], ("col", "row"), axis=0)
    x_all = x_all.reshape(C, R * patches.shape[1], patches.shape[2])
    patch_total = x_all.shape[1]
    head_of = c * hr // C
    small = lax.all_gather(jnp.stack([vis_gain, vis_bias]), "col", axis=0)
    wv = lax.all_gather(vis_qkv, "col", axis=0)
    wv = lax.dynamic_slice_in_dim(wv, head_of * 3 * HEAD_DIM, 3 * HEAD_DIM, axis=2)
    wv = pad_parts(wv)
    wvb = pad_parts(lax.dynamic_slice_in_dim(vis_qkv_bias, head_of * 3 * HEAD_DIM, 3 * HEAD_DIM, 0))
    text_all = lax.all_gather(text, ("col", "row"), axis=0).reshape(C, R, own_text, text.shape[1])
    vis_out_all = lax.all_gather(vis_out, "row", axis=0, tiled=True)
    wd = jnp.transpose(dec_qkv.reshape(dec_qkv.shape[0], hc, 3 * HEAD_DIM), (1, 0, 2))
    wd = pad_parts(jnp.repeat(wd, share, axis=0) if share > 1 else wd)
    wd = lax.all_to_all(wd, "row", 0, 0)
    dec_out_all = lax.all_gather(dec_out, ("col", "row"), axis=0)
    dec_out_all = dec_out_all.reshape(C, R, hc, HEAD_DIM, dec_out.shape[1])
    gain_all = lax.all_gather(dec_gain, "row", axis=0)[:, None]

    patch_ids = segment_of(jnp.arange(patch_total, dtype=jnp.int32) // 4, image_lengths)
    attn = vis_head(x_all, small[:, :1], small[:, 1:], wv, wvb[None], patch_ids, scale)
    attn_all = lax.all_gather(attn[:, :HEAD_DIM], ("row", "col"), axis=0)
    attn_all = attn_all.reshape(R, C, patch_total, HEAD_DIM)[:, :: C // hr]
    attn_all = jnp.transpose(attn_all, (2, 0, 1, 3)).reshape(patch_total, HEADS * HEAD_DIM)
    own_x = lax.dynamic_index_in_dim(x_all, c, 0, keepdims=False)
    resid = (
        own_x.astype(F32)
        + jnp.dot(attn_all, vis_out_all, preferred_element_type=F32)
        + vis_out_bias.astype(F32)
    ).astype(BF16)
    merged = resid.reshape(patch_total // 4, 4 * resid.shape[1])
    partial = jnp.dot(
        merged, proj_weight.reshape(4 * proj_weight.shape[1], -1), preferred_element_type=F32
    )
    image_rows = (lax.psum(partial, "col") + proj_bias.astype(F32)).astype(BF16)
    image_all = lax.all_gather(image_rows, "row", axis=0)

    text_qkv = dec_rows(text_all, gain_all, wd, TPD).reshape(half_rows, 3 * PAD)
    image_qkv = dec_rows(image_all[None], gain_all, wd, image_rows.shape[0])[0]
    source, inside = insert_map(jnp.arange(half_rows, dtype=jnp.int32), image_lengths, gaps)
    pick = jnp.where(inside, source, -1)
    hot = (pick[:, None] == jnp.arange(image_rows.shape[0], dtype=jnp.int32)[None]).astype(BF16)
    placed = jnp.dot(hot, image_qkv, preferred_element_type=F32).astype(BF16)
    qkv = jnp.where(inside[:, None], placed, text_qkv)
    both = lax.all_gather(qkv[:, PAD:], "grp", axis=0)
    t = jnp.arange(half_rows, dtype=jnp.int32)
    at = t // TPD * (2 * TPD) + g * TPD + t % TPD
    begin = starts_of(at, doc_lengths)
    out = dec_attn(qkv[:, :PAD], both[..., :PAD], both[..., PAD:], begin, at, scale)

    mine = half_rows // (C * R)
    spread = out[:, :HEAD_DIM].reshape(C * R, mine, HEAD_DIM)
    rows = lax.all_to_all(spread, ("col", "row"), 0, 0)
    rows = rows.reshape(C, R, mine, HEAD_DIM)[:, ::share]
    delta = jnp.einsum(
        "chte,crhef->rtf", rows, dec_out_all, preferred_element_type=F32
    ).astype(BF16)
    delta = lax.all_to_all(delta, "row", 0, 0).reshape(own_text, text.shape[1])
    own_hot = lax.dynamic_slice_in_dim(hot, c * own_text, own_text, 0)
    own_inside = lax.dynamic_slice_in_dim(inside, c * own_text, own_text, 0)
    own_placed = jnp.dot(own_hot, image_rows, preferred_element_type=F32)
    dec_input = jnp.where(own_inside[:, None], own_placed, text.astype(F32))
    return (dec_input + delta.astype(F32)).astype(BF16)[None]


def solution(mesh):
    return jax.shard_map(
        per_device,
        mesh=mesh,
        in_specs=(
            P("grp", "row", "col"),
            P("col"),
            P("col"),
            P("col", "row"),
            P("row"),
            P("row", "col"),
            P("col"),
            P(None, "col", "row"),
            P("row"),
            P("grp", "col", "row"),
            P("row"),
            P("row", "col"),
            P("col", "row"),
            P("grp", None),
            P("grp", None),
            P(),
        ),
        out_specs=P("grp", "col", "row"),
        check_vma=False,
    )
```

time: 858 us -> 408 us (0.48)
  waiting for transfers between devices: 608 us -> 220 us
  matrix products: 69.1 us -> 13.8 us
  Pallas kernels: 0 us -> 25.4 us
  blocking collectives: 96.5 us -> 71.3 us
  other arithmetic: 27.7 us -> 3.15 us
  starting transfers between devices: 0.43 us -> 13 us
    reduce_scatter x5 -> x0, waiting for transfers between devices: 378 us -> none  [the longest x1 291 us: per_device(): lax.psum_scatter(product_rows(gathered_text, dec_qkv)(jnp.int32(0), lax.a...]
    dot_general x23 -> x5, matrix products: 69.1 us -> 13.8 us  [the longest x1 5.62 us: per_device(): jnp.einsum('chte,crhef->rtf', rows, dec_out_all, preferred_element_type=F32)]
    all_gather x5 -> x2, blocking collectives: 72.3 us -> 41 us  [the longest x1 39.1 us: per_device(): image_all = lax.all_gather(image_rows, 'row', axis=0)]
    unnamed x0 -> x1, blocking collectives: none -> 30.3 us
    pallas_call x0 -> x4, Pallas kernels: none -> 25.4 us  [the longest x1 11.8 us: dec_attn(): pl.pallas_call(functools.partial(dec_attn_kernel, scale=scale), grid_spec...]
    psum x2 -> x0, blocking collectives: 24.2 us -> none  [the longest x1 21.6 us: per_device(): squares = lax.psum(jnp.sum(xdec * xdec, axis=1), 'row')]
    all_gather x2 -> x7, waiting for transfers between devices: 230 us -> 206 us  [the longest x1 47.8 us: per_device(): vis_out_all = lax.all_gather(vis_out, 'row', axis=0, tiled=True)]
    reshape x2 -> x8, local copies, waits for them, and re-layouts: 1.04 us -> 20.9 us  [the longest x1 10.8 us: per_device(): dec_out_all = dec_out_all.reshape(C, R, hc, HEAD_DIM, dec_out.shape[1])]
  transfers between devices with their start and end apart: 7 -> 11, of which waited for: 7 -> 8; matrix products, arithmetic and copies ran while one was open for 0% -> 8% of each run, Pallas kernels for 0% -> 3%
where the time goes in v1:
time: 408 us; the launch traced here: 407 us
  waiting for transfers between devices  220 us (54%)
  blocking collectives  71.3 us (17%)
  local copies, waits for them, and re-layouts  45.3 us (11%)
  Pallas kernels  25.4 us (6%)
  between operations  14.5 us (4%)
  matrix products  13.8 us (3%)
  starting transfers between devices  13 us (3%)
    all_gather x1, waiting for transfers between devices, per_device(): vis_out_all = lax.all_gather(vis_out, 'row', axis=0, tiled=True)  47.8 us
    all_gather x1, waiting for transfers between devices, per_device(): x_all = lax.all_gather(patches[0], ('col', 'row'), axis=0)  41.1 us
    all_gather x1, blocking collectives, per_device(): image_all = lax.all_gather(image_rows, 'row', axis=0)  39.1 us
    all_gather x1, waiting for transfers between devices, per_device(): dec_out_all = lax.all_gather(dec_out, ('col', 'row'), axis=0)  37.4 us
    all_gather x1, waiting for transfers between devices, per_device(): attn_all = lax.all_gather(attn[:, :HEAD_DIM], ('row', 'col'), axis=0)  37.4 us
    unnamed x1, blocking collectives  30.3 us
    all_gather x1, waiting for transfers between devices, per_device(): both = lax.all_gather(qkv[:, PAD:], 'grp', axis=0)  29.5 us
    pallas_call x1, Pallas kernels, dec_attn(): pl.pallas_call(functools.partial(dec_attn_kernel, scale=scale), grid_spec...  11.8 us
  transfers between devices with their start and end apart: 11, of which 8 were waited for; matrix products, arithmetic and copies ran while one was open for 8% of the time, Pallas kernels for 3%

profile of v1, /device:TPU:0, one launch (start us, length us, event | category | flops | bytes accessed | tf_op | source)
XLA Modules:
  0.0 406.7 jit_solution(7406451283402493281)
XLA Ops:
  6.5 0.7 all-gather.28.cloned.1.call-update
  7.3 0.7 all-gather.18.cloned.1.call-update
  8.1 0.7 stack.10
  8.7 0.7 stack.9
  9.4 0.8 dynamic_slice.20
  10.3 0.8 reduce-window.19
  11.4 1.9 all-gather.7
  13.3 8.2 %all-gather.28.cloned.1.call-done = bf16[2,704,528]{1,2,0:T(8,128)(2,1)} async-done(((bf16[1,704,528]{1,2,0:T(8,128)(2,1)}), bf16[2,704,528]{1,2,0:T(8,128)(2,1)}) %all-gather.28.cloned.1.call-update) | async-done | bytes 1486864 | tf_op jit(solution)/shard_map/all_gather | solution.py:218
  21.5 1.2 constant_dynamic-slice_fusion
  22.8 0.7 copy.53.w_ref
  23.5 41.1 %all-gather.18.cloned.1.call-done = bf16[16,64,704]{2,1,0:T(8,128)(2,1)} async-done(((bf16[1,64,704]{2,1,0:T(8,128)(2,1)}), bf16[16,64,704]{2,1,0:T(8,128)(2,1)}) %all-gather.18.cloned.1.call-update) | async-done | bytes 1441808 | tf_op jit(solution)/shard_map/all_gather | solution.py:213
  64.6 1.4 copy-done
  66.0 3.0 vis_head.1
  69.7 0.6 copy.57
  70.3 1.9 reshape.191
  72.1 37.4 %all-gather.24.cloned.1.call-done = bf16[8192,88]{1,0:T(8,128)(2,1)} async-done(((bf16[512,88]{1,0:T(8,128)(2,1)}), bf16[8192,88]{1,0:T(8,128)(2,1)}) %all-gather.24.cloned.1.call-update) | async-done | bytes 1441808 | tf_op jit(solution)/shard_map/all_gather | solution.py:233
  109.5 3.0 copy.55
  112.5 47.8 %all-gather.20.cloned.1.call-done = bf16[1408,704]{1,0:T(8,128)(2,1)} async-done(((bf16[176,704]{1,0:T(8,128)(2,1)}), bf16[1408,704]{1,0:T(8,128)(2,1)}) %all-gather.20.cloned.1.call-update) | async-done | bytes 1982480 | tf_op jit(solution)/shard_map/all_gather | solution.py:223
  160.3 3.9 fusion.8
  164.2 2.0 reshape.190
  166.3 1.1 fusion.49
  168.0 1.1 copy.59
  169.3 1.5 copy.71
  170.9 3.7 all-to-all-start
  174.8 0.6 dynamic-slice
  176.4 30.3 %all-reduce.3 = bf16[1408]{0:T(1024)(128)(2,1)S(1)} all-reduce(bf16[1408]{0:T(1024)(128)(2,1)S(1)} %dynamic-update-slice), channel_id=6, replica_groups=mesh['row'=8,'col'=2,'grp'=2] {'row'}, use_global_device_ids=true, to_apply=%add.3 | all-reduce | flops 1408 | bytes 5632
  207.0 1.0 add_convert_fusion
  208.0 39.1 %all-gather.3 = bf16[1024,176]{0,1:T(8,128)(2,1)S(1)} all-gather(bf16[128,176]{0,1:T(8,128)(2,1)S(1)} %add_convert_fusion), channel_id=5, replica_groups=mesh['row'=8,'col'=2,'grp'=2] {'row'}, dimensions={0}, use_global_device_ids=true | all-gather | bytes 405504 | tf_op jit(solution)/shard_map/all_gather | solution.py:247
  247.3 0.6 dec_rows.2
  247.9 4.3 %all-gather.22.cloned.1.call-done = bf16[16,1024,176]{1,2,0:T(8,128)(2,1)} async-done(((bf16[1,1024,176]{1,2,0:T(8,128)(2,1)}), bf16[16,1024,176]{1,2,0:T(8,128)(2,1)}) %all-gather.22.cloned.1.call-update) | async-done | bytes 5767184 | tf_op jit(solution)/shard_map/all_gather | solution.py:222
  252.2 10.9 %copy.62 = bf16[16,1024,176]{2,1,0:T(8,128)(2,1)} copy(bf16[16,1024,176]{1,2,0:T(8,128)(2,1)} %all-gather.22.cloned.1.call-done) | data formatting | bytes 11534336 | tf_op jit(solution)/shard_map/all_gather | solution.py:222
  263.1 10.0 %dec_rows.3 = bf16[2,1024,384]{2,1,0:T(8,128)(2,1)S(1)} custom-call(bf16[2,8,1024,176]{3,2,1,0:T(8,128)(2,1)} %bitcast.111, bf16[8,1,176]{2,1,0:T(2,128)(2,1)S(1)} %broadcast_in_dim.88.gain_ref, bf16[8,176,384]{2,1,0:T(8,128)(2,1)S(1)} %all-to-all-done.w_ref), custom_call_target="tpu_custom_call" | custom-call | tf_op jit(solution)/shard_map/dec_rows/pallas_call | solution.py:101
  273.1 2.1 fusion.2
  275.2 1.1 copy-done.2
  276.4 1.0 slice.48
  277.5 0.7 all-gather.30.cloned.1.call-update
  279.2 1.1 slice.47.q_ref
  280.3 29.5 %all-gather.26.cloned.1.call-done = bf16[4096,256]{1,0:T(8,128)(2,1)} async-done(((bf16[2048,256]{1,0:T(8,128)(2,1)}), bf16[4096,256]{1,0:T(8,128)(2,1)}) %all-gather.26.cloned.1.call-update) | async-done | bytes 2097168 | tf_op jit(solution)/shard_map/all_gather | solution.py:256
  309.8 1.7 fusion.47
  311.5 11.8 %dec_attn.1 = bf16[2048,128]{1,0:T(8,128)(2,1)S(1)} custom-call(s32[8]{0:T(128)S(1)} %and_select_fusion.low_ref, bf16[2048,128]{1,0:T(8,128)(2,1)S(1)} %slice.47.q_ref, s32[2048,1]{1,0:T(8,128)S(1)} %copy.64.start_ref, s32[2048,1]{1,0:T(8,128)S(1)} %fusion.25.pos_ref, bf16[2,2048,128]{2,1,0:T(8,128)(2,1)S(1)} %get-tuple-element.6.k_ref, ...), custom_call_target="tpu_custom_call" | custom-call | tf_op jit(solution)/shard_map/dec_attn/pallas_call | solution.py:153
  323.3 0.9 copy.65
  324.2 5.6 %all-to-all-start.1 = ((bf16[16,128,88]{1,2,0:T(8,128)(2,1)}), bf16[16,128,88]{1,2,0:T(8,128)(2,1)S(1)}, u32[]{:S(2)}, u32[]{:S(2)}) async-start(bf16[16,128,88]{1,2,0:T(8,128)(2,1)} %copy.65), calls=%async_computation.1 | async-start | bytes 720896 | tf_op jit(solution)/shard_map/all_to_all | solution.py:264
  329.9 37.4 %all-gather.30.cloned.1.call-done = bf16[16,704,176]{1,2,0:T(8,128)(2,1)} async-done(((bf16[1,704,176]{1,2,0:T(8,128)(2,1)}), bf16[16,704,176]{1,2,0:T(8,128)(2,1)}) %all-gather.30.cloned.1.call-update) | async-done | bytes 3964944 | tf_op jit(solution)/shard_map/all_gather | solution.py:227
  367.3 10.8 %reshape.201 = bf16[2,8,8,88,176]{3,2,4,1,0:T(8,128)(2,1)} reshape(bf16[16,704,176]{1,2,0:T(8,128)(2,1)} %all-gather.30.cloned.1.call-done) | data formatting | bytes 7929856 | tf_op jit(solution)/shard_map/reshape | solution.py:228
  378.1 5.6 %fusion.17 = bf16[8,128,176]{1,2,0:T(8,128)(2,1)} fusion(bf16[2,8,128,88,1]{2,3,1,4,0:T(8,128)(2,1)S(1)} %bitcast.120, bf16[2,8,8,88,176]{3,2,4,1,0:T(8,128)(2,1)} %reshape.201), kind=kOutput, calls=%fused_computation.20 | convolution fusion | flops 507691008 | bytes 4685824 | tf_op jit(solution)/shard_map/chte,crhef->rtf/dot_general | solution.py:266
  383.8 3.4 all-to-all-start.2
  387.6 11.2 %all-to-all-done.2 = bf16[8,128,176]{1,2,0:T(8,128)(2,1)S(1)} async-done(((bf16[8,128,176]{1,2,0:T(8,128)(2,1)}), bf16[8,128,176]{1,2,0:T(8,128)(2,1)S(1)}, u32[]{:S(2)}, u32[]{:S(2)}) %all-to-all-start.2) | async-done | bytes 360480 | tf_op jit(solution)/shard_map/all_to_all | solution.py:269
  398.8 1.0 fusion.20
  (72 shorter events, 4.4 us)
Async XLA Ops:
  6.5 15.0 %all-gather.28.cloned.1.call-start = ((), (), s32[]{:S(2)}) async-start(), calls=%async_computation.9 | async-start | bytes 2433024 | tf_op jit(solution)/shard_map/all_gather | solution.py:218
  7.3 57.4 %all-gather.18.cloned.1.call-start = ((), (), s32[]{:S(2)}) async-start(), calls=%async_computation.3 | async-start | bytes 1671168 | tf_op jit(solution)/shard_map/all_gather | solution.py:213
  8.0 101.5 %all-gather.24.cloned.1.call-start = ((), (), s32[]{:S(2)}) async-start(), calls=%async_computation.7 | async-start | bytes 2228224 | tf_op jit(solution)/shard_map/all_gather | solution.py:233
  64.6 1.4 copy-start
  66.0 3.6 copy-start.7
  66.0 3.6 copy-start.5
  69.0 91.3 %all-gather.20.cloned.1.call-start = ((), (), s32[]{:S(2)}) async-start(), calls=%async_computation.4 | async-start | bytes 2433024 | tf_op jit(solution)/shard_map/all_gather | solution.py:223
  69.6 137.4 %all-reduce.6.cloned.1.call-start = ((), (), s32[]{:S(2)}) async-start(), calls=%async_computation.5 | async-start | bytes 180224 | tf_op jit(solution)/shard_map/psum | solution.py:246
  109.5 50.8 %copy-start.1 = (bf16[16,64,704]{2,1,0:T(8,128)(2,1)S(1)}, bf16[16,64,704]{2,1,0:T(8,128)(2,1)}, u32[]{:S(2)}) copy-start(bf16[16,64,704]{2,1,0:T(8,128)(2,1)} %all-gather.18.cloned.1.call-done) | copy-start | bytes 4325380
  164.2 2.1 copy-start.3
  164.2 3.7 copy-start.6
  167.4 84.8 %all-gather.22.cloned.1.call-start = ((), (), s32[]{:S(2)}) async-start(), calls=%async_computation.6 | async-start | bytes 6127616 | tf_op jit(solution)/shard_map/all_gather | solution.py:222
  170.8 3.8 copy-start.10
  170.8 3.8 copy-start.11
  170.8 4.0 copy-start.13
  170.8 5.3 %copy-start.12 = (bf16[176]{0:T(256)(128)(2,1)S(1)}, bf16[176]{0:T(256)(128)(2,1)}, u32[]{:S(2)}) copy-start(bf16[176]{0:T(256)(128)(2,1)} %param.26) | copy-start | bytes 1060
  170.8 35.9 %copy-start.9 = (s32[1,8]{1,0:T(1,128)S(1)}, s32[1,8]{1,0:T(1,128)}, u32[]{:S(2)}) copy-start(s32[1,8]{1,0:T(1,128)} %param.29) | copy-start | bytes 100
  170.9 76.4 %all-to-all-start = ((bf16[8,176,384]{2,1,0:T(8,128)(2,1)}), bf16[8,176,384]{2,1,0:T(8,128)(2,1)S(1)}, u32[]{:S(2)}, u32[]{:S(2)}) async-start(bf16[8,176,384]{2,1,0:T(8,128)(2,1)} %copy.71), calls=%async_computation | async-start | bytes 2162688 | tf_op jit(solution)/shard_map/all_to_all | solution.py:226
  174.6 135.2 %all-gather.26.cloned.1.call-start = ((), (), s32[]{:S(2)}) async-start(), calls=%async_computation.8 | async-start | bytes 3145728 | tf_op jit(solution)/shard_map/all_gather | solution.py:256
  275.2 1.1 copy-start.2
  276.4 1.8 copy-start.8
  277.4 89.9 %all-gather.30.cloned.1.call-start = ((), (), s32[]{:S(2)}) async-start(), calls=%async_computation.10 | async-start | bytes 4595712 | tf_op jit(solution)/shard_map/all_gather | solution.py:227
  324.2 53.9 %all-to-all-start.1 = ((bf16[16,128,88]{1,2,0:T(8,128)(2,1)}), bf16[16,128,88]{1,2,0:T(8,128)(2,1)S(1)}, u32[]{:S(2)}, u32[]{:S(2)}) async-start(bf16[16,128,88]{1,2,0:T(8,128)(2,1)} %copy.65), calls=%async_computation.1 | async-start | bytes 720896 | tf_op jit(solution)/shard_map/all_to_all | solution.py:264
  378.1 20.7 %copy-start.4 = (bf16[1,1024,176]{1,2,0:T(8,128)(2,1)S(1)}, bf16[1,1024,176]{1,2,0:T(8,128)(2,1)}, u32[]{:S(2)}) copy-start(bf16[1,1024,176]{1,2,0:T(8,128)(2,1)} %param.25) | copy-start | bytes 1081348
  383.8 15.0 %all-to-all-start.2 = ((bf16[8,128,176]{1,2,0:T(8,128)(2,1)}), bf16[8,128,176]{1,2,0:T(8,128)(2,1)S(1)}, u32[]{:S(2)}, u32[]{:S(2)}) async-start(bf16[8,128,176]{1,2,0:T(8,128)(2,1)} %fusion.17), calls=%async_computation.2 | async-start | bytes 720896 | tf_op jit(solution)/shard_map/all_to_all | solution.py:269
Sparse Core Ops, SparseCore 0:
  8.9 12.5 all-gather.27
  23.7 40.8 all-gather.17
  69.2 40.2 all-gather.23
  111.5 48.7 all-gather.19
  167.5 16.2 all-reduce.5
  185.9 66.2 all-gather.21
  277.6 32.2 all-gather.25
  312.0 55.2 all-gather.29

commit v2 on v1

--- a/solution.py
+++ b/solution.py
@@ -41,24 +41,156 @@
     return (source, jnp.any(inside, axis=1))
 
 
-def vis_head_kernel(
-    x_ref, gain_ref, bias_ref, w_ref, wb_ref, ids_ref, idk_ref, o_ref, *, scale, width
+class Links:
+    def __init__(self, send, recv, rows, cols):
+        self.send, self.recv = send, recv
+        self.rows, self.cols = rows, cols
+        self.r, self.c = lax.axis_index("row"), lax.axis_index("col")
+        self.g = lax.axis_index("grp")
+        self.high, self.low = self.r // 2, self.r % 2
+        self.count = 0
+        self.taken = 0
+        self.pending = []
+
+    def slots(self, number):
+        base = self.taken
+        self.taken += number
+        return base
+
+    def push(self, src, dst, slot, **where):
+        copy = pltpu.make_async_remote_copy(
+            src_ref=src,
+            dst_ref=dst,
+            send_sem=self.send.at[self.count],
+            recv_sem=self.recv.at[slot],
+            device_id=where,
+            device_id_type=pl.DeviceIdType.MESH,
+        )
+        self.count += 1
+        copy.start()
+        self.pending.append(copy)
+
+    def arrived(self, dst, slot):
+        pltpu.make_async_remote_copy(
+            src_ref=dst,
+            dst_ref=dst,
+            send_sem=self.send.at[0],
+            recv_sem=self.recv.at[slot],
+            device_id={"row": self.r},
+            device_id_type=pl.DeviceIdType.MESH,
+        ).wait_recv()
+
+    def row_peer(self, step):
+        return (self.high + step) % (self.rows // 2) * 2 + self.low
+
+    def row_start(self, src, dst, base):
+        other = self.high * 2 + 1 - self.low
+        for step in range(1, self.rows // 2):
+            self.push(src, dst.at[self.r], base + self.r, row=self.row_peer(step))
+        self.push(src, dst.at[self.r], base + self.r, row=other)
+
+    def row_forward(self, dst, base):
+        other = self.high * 2 + 1 - self.low
+        for step in range(1, self.rows // 2):
+            at = self.row_peer(self.rows // 2 - step)
+            self.arrived(dst.at[at], base + at)
+            self.push(dst.at[at], dst.at[at], base + at, row=other)
+
+    def row_finish(self, dst, base):
+        for step in range(self.rows // 2):
+            at = (self.high + step) % (self.rows // 2) * 2 + 1 - self.low
+            self.arrived(dst.at[at], base + at)
+
+    def col_start(self, src, dst, base):
+        for step in range(1, self.cols):
+            self.push(src, dst, base + self.c, col=(self.c + step) % self.cols)
+
+    def col_finish(self, dst, base):
+        for step in range(1, self.cols):
+            at = (self.c + step) % self.cols
+            self.arrived(dst.at[at], base + at)
+
+
+def front_kernel(
+    patch_ref, small_ref, wv_in, wvb_ref, ids_ref, idk_ref, vo_in, vob_ref, proj_ref, projb_ref,
+    text_in, gain_in, wd_in, meta_in,
+    qkv_ref, img_ref, image_ref, meta_ref,
+    x_ref, s_ref, wv_ref, vo_ref, wd_ref, gain_ref, text_ref, at_ref, part_ref,
+    send, recv, local,
+    *, rows, cols, hr, scale, width,
 ):
-    parts, count = x_ref.shape[0], x_ref.shape[1]
+    net = Links(send, recv, rows, cols)
+    r, c, g = net.r, net.c, net.g
+    barrier = pltpu.get_barrier_semaphore()
+    for step in range(1, rows):
+        pl.semaphore_signal(barrier, inc=1, device_id={"row": (r + step) % rows},
+                            device_id_type=pl.DeviceIdType.MESH)
+    for step in range(1, cols):
+        pl.semaphore_signal(barrier, inc=1, device_id={"col": (c + step) % cols},
+                            device_id_type=pl.DeviceIdType.MESH)
+    pl.semaphore_signal(barrier, inc=1, device_id={"grp": 1 - g},
+                        device_id_type=pl.DeviceIdType.MESH)
+    pl.semaphore_wait(barrier, rows + cols - 1)
+
+    own = [
+        (patch_ref, x_ref.at[c, r]),
+        (small_ref, s_ref.at[c]),
+        (wv_in.at[c * hr // cols], wv_ref.at[c]),
+        (vo_in, vo_ref.at[r]),
+        (wd_in.at[r], wd_ref.at[r]),
+        (gain_in, gain_ref.at[r]),
+        (text_in, text_ref.at[c, r]),
+        (meta_in, meta_ref.at[g]),
+    ]
+    own = [pltpu.make_async_copy(a, b, local.at[i]) for i, (a, b) in enumerate(own)]
+    for copy in own:
+        copy.start()
+
+    x_row, x_col = net.slots(rows), net.slots(cols)
+    s_col, wv_col = net.slots(cols), net.slots(cols)
+    vo_row, wd_row, gain_row = net.slots(rows), net.slots(rows), net.slots(rows)
+    text_row, text_col = net.slots(rows), net.slots(cols)
+    at_row, at_col = net.slots(rows), net.slots(cols)
+    part_col, img_row, meta_grp = net.slots(cols), net.slots(rows), net.slots(1)
+    kv_grp, imgkv_grp = net.slots(1), net.slots(1)
+
+    net.row_start(patch_ref, x_ref.at[c], x_row)
+    net.col_start(small_ref, s_ref.at[c], s_col)
+    for step in range(1, cols):
+        to = (c + step) % cols
+        net.push(wv_in.at[to * hr // cols], wv_ref.at[c], wv_col + c, col=to)
+    net.push(meta_in, meta_ref.at[g], meta_grp, grp=1 - g)
+    net.row_start(gain_in, gain_ref, gain_row)
+    net.row_start(text_in, text_ref.at[c], text_row)
+    net.row_start(vo_in, vo_ref, vo_row)
+    for step in range(1, rows):
+        to = (r + step) % rows
+        net.push(wd_in.at[to], wd_ref.at[r], wd_row + r, row=to)
+    for copy in own:
+        copy.wait()
+    net.row_forward(x_ref.at[c], x_row)
+    net.row_finish(x_ref.at[c], x_row)
+    net.col_start(x_ref.at[c], x_ref.at[c], x_col)
+    net.col_finish(s_ref, s_col)
+    net.col_finish(wv_ref, wv_col)
+    net.col_finish(x_ref, x_col)
+
+    count = rows * patch_ref.shape[0]
+    depth = patch_ref.shape[1]
     one = jnp.zeros((count, 1), F32)
     two = jnp.zeros((count, 1), F32)
-    for c in range(parts):
-        x = x_ref[c].astype(F32)
+    for i in range(cols):
+        x = x_ref[i].reshape(count, depth).astype(F32)
         one += jnp.sum(x, axis=1, keepdims=True)
         two += jnp.sum(x * x, axis=1, keepdims=True)
     mean = one / width
     inv = lax.rsqrt(two / width - mean * mean + 1e-06)
     qkv = jnp.zeros((count, 3 * PAD), F32)
-    for c in range(parts):
-        x = x_ref[c].astype(F32)
-        normed = ((x - mean) * inv * gain_ref[c].astype(F32) + bias_ref[c].astype(F32)).astype(BF16)
-        qkv += jnp.dot(normed, w_ref[c], preferred_element_type=F32)
-    qkv = (qkv + wb_ref[...].astype(F32)).astype(BF16)
+    for i in range(cols):
+        x = x_ref[i].reshape(count, depth).astype(F32)
+        normed = ((x - mean) * inv * s_ref[i, 0:1] + s_ref[i, 1:2]).astype(BF16)
+        qkv += jnp.dot(normed, wv_ref[i], preferred_element_type=F32)
+    qkv = (qkv + wvb_ref[...].astype(F32)).astype(BF16)
     q, k, v = qkv[:, :PAD], qkv[:, PAD : 2 * PAD], qkv[:, 2 * PAD :]
     scores = lax.dot_general(q, k, (((1,), (1,)), ((), ())), preferred_element_type=F32)
     scores = scores * (scale * LOG2E)
@@ -68,49 +200,126 @@
     weights = jnp.where(allowed, jnp.exp2(scores - top), 0.0)
     total = jnp.sum(weights, axis=1, keepdims=True)
     mixed = jnp.dot(weights.astype(BF16), v, preferred_element_type=F32) / total
-    o_ref[...] = mixed.astype(BF16)
-
-
-def vis_head(x, gain, bias, w, wb, ids, scale):
-    count = x.shape[1]
+    mine = c * hr // cols
+    at_ref[mine, r] = mixed.astype(BF16)
+    net.row_start(at_ref.at[mine, r], at_ref.at[mine], at_row)
+    net.row_forward(at_ref.at[mine], at_row)
+    net.row_forward(text_ref.at[c], text_row)
+    net.row_finish(at_ref.at[mine], at_row)
+    for step in range(1, hr):
+        to = (c + step * (cols // hr)) % cols
+        net.push(at_ref.at[mine], at_ref.at[mine], at_col + mine, col=to)
+    net.row_forward(vo_ref, vo_row)
+    net.row_finish(vo_ref, vo_row)
+    for step in range(1, hr):
+        other = (mine + step) % hr
+        net.arrived(at_ref.at[other], at_col + other)
+
+    delta = x_ref[c].reshape(count, depth).astype(F32) + vob_ref[...].astype(F32)
+    for i in range(rows):
+        for h in range(hr):
+            delta += jnp.dot(at_ref[h, i], vo_ref[i, h], preferred_element_type=F32)
+    tokens = count // 4
+    resid = delta.astype(BF16).reshape(rows, 4, tokens // rows, depth)
+    partial = jnp.zeros(part_ref.shape[1:], F32)
+    for i in range(4):
+        quarter = resid[:, i].reshape(tokens, depth)
+        partial += jnp.dot(quarter, proj_ref[i], preferred_element_type=F32)
+    part_ref[c] = partial
+    net.col_start(part_ref.at[c], part_ref.at[c], part_col)
+    net.col_finish(part_ref, part_col)
+    image = projb_ref[...].astype(F32)
+    for i in range(cols):
+        image = image + part_ref[i]
+    image_ref[r] = image.astype(BF16)
+    net.row_start(image_ref.at[r], image_ref, img_row)
+    net.row_forward(gain_ref, gain_row)
+    net.row_finish(gain_ref, gain_row)
+    net.row_finish(text_ref.at[c], text_row)
+    net.col_start(text_ref.at[c], text_ref.at[c], text_col)
+    for step in range(1, rows):
+        at = (r + step) % rows
+        net.arrived(wd_ref.at[at], wd_row + at)
+    net.row_forward(image_ref, img_row)
+
+    def head_rows(part):
+        number = part(0).shape[0]
+        squares = jnp.zeros((number, 1), F32)
+        for i in range(rows):
+            x = part(i).astype(F32)
+            squares += jnp.sum(x * x, axis=1, keepdims=True)
+        inv = lax.rsqrt(squares / width + 1e-05)
+        total = jnp.zeros((number, 3 * PAD), F32)
+        for i in range(rows):
+            normed = (part(i).astype(F32) * inv * gain_ref[i, 0:1]).astype(BF16)
+            total += jnp.dot(normed, wd_ref[i], preferred_element_type=F32)
+        return total.astype(BF16)
+
+    own_rows = text_in.shape[0]
+
+    def text_block(at):
+        @pl.loop(0, own_rows // TPD)
+        def _(j):
+            start = pl.multiple_of(j * TPD, TPD)
+            found = head_rows(lambda i: text_ref[at, i, pl.ds(start, TPD)])
+            qkv_ref[g, pl.ds(pl.multiple_of(at * own_rows + start, TPD), TPD)] = found
+
+    text_block(c)
+    net.row_finish(image_ref, img_row)
+    img_ref[g] = head_rows(lambda i: image_ref[i])
+    net.push(img_ref.at[g], img_ref.at[g], imgkv_grp, grp=1 - g)
+    net.col_finish(text_ref, text_col)
+    for step in range(1, cols):
+        text_block((c + step) % cols)
+    net.push(qkv_ref.at[g], qkv_ref.at[g], kv_grp, grp=1 - g)
+    net.arrived(meta_ref.at[1 - g], meta_grp)
+    net.arrived(img_ref.at[1 - g], imgkv_grp)
+    net.arrived(qkv_ref.at[1 - g], kv_grp)
+    for copy in net.pending:
+        copy.wait_send()
+
+
+def front(patch, small, wv, wvb, ids, vo, vob, proj, projb, text, gain, wd, meta, rows, cols, scale):
+    hr = wv.shape[0]
+    count = rows * patch.shape[0]
+    half = cols * text.shape[0]
+    tokens = count // 4
+    depth = proj.shape[2]
+    args = (patch, small, wv, wvb, ids[:, None], ids[None, :], vo, vob, proj, projb, text, gain, wd, meta)
+    sends = 6 * (rows - 1) + (rows - 1) + 6 * (cols - 1) + 3
+    slots = 7 * rows + 6 * cols + 3
+    vmem = pl.BlockSpec(memory_space=pltpu.VMEM)
     return pl.pallas_call(
-        functools.partial(vis_head_kernel, scale=scale, width=HEADS * HEAD_DIM),
-        out_shape=jax.ShapeDtypeStruct((count, PAD), BF16),
-        compiler_params=pltpu.CompilerParams(vmem_limit_bytes=48 << 20),
-        name="vis_head",
-    )(x, gain, bias, w, wb, ids[:, None], ids[None, :])
-
-
-def dec_qkv_kernel(x_ref, gain_ref, w_ref, o_ref, *, width):
-    parts, count = x_ref.shape[1], x_ref.shape[2]
-    squares = jnp.zeros((count, 1), F32)
-    for r in range(parts):
-        x = x_ref[0, r].astype(F32)
-        squares += jnp.sum(x * x, axis=1, keepdims=True)
-    inv = lax.rsqrt(squares / width + 1e-05)
-    qkv = jnp.zeros((count, 3 * PAD), F32)
-    for r in range(parts):
-        x = x_ref[0, r].astype(F32)
-        normed = (x * inv * gain_ref[r].astype(F32)).astype(BF16)
-        qkv += jnp.dot(normed, w_ref[r], preferred_element_type=F32)
-    o_ref[0] = qkv.astype(BF16)
-
-
-def dec_rows(x, gain, w, tile):
-    groups, parts, count, depth = x.shape
-    return pl.pallas_call(
-        functools.partial(dec_qkv_kernel, width=HEADS * HEAD_DIM),
-        grid=(groups, count // tile),
-        in_specs=[
-            pl.BlockSpec((1, parts, tile, depth), lambda i, j: (i, 0, j, 0)),
-            pl.BlockSpec(gain.shape, lambda i, j: (0, 0, 0)),
-            pl.BlockSpec(w.shape, lambda i, j: (0, 0, 0)),
+        functools.partial(
+            front_kernel, rows=rows, cols=cols, hr=hr, scale=scale, width=HEADS * HEAD_DIM
+        ),
+        in_specs=[vmem] * len(args),
+        out_specs=[vmem] * 4,
+        out_shape=[
+            jax.ShapeDtypeStruct((2, half, 3 * PAD), BF16),
+            jax.ShapeDtypeStruct((2, tokens, 3 * PAD), BF16),
+            jax.ShapeDtypeStruct((rows, tokens, depth), BF16),
+            jax.ShapeDtypeStruct((2,) + meta.shape, jnp.int32),
         ],
-        out_specs=pl.BlockSpec((1, tile, 3 * PAD), lambda i, j: (i, j, 0)),
-        out_shape=jax.ShapeDtypeStruct((groups, count, 3 * PAD), BF16),
-        compiler_params=pltpu.CompilerParams(vmem_limit_bytes=48 << 20),
-        name="dec_rows",
-    )(x, gain, w)
+        scratch_shapes=[
+            pltpu.VMEM((cols, rows) + patch.shape, BF16),
+            pltpu.VMEM((cols,) + small.shape, F32),
+            pltpu.VMEM((cols,) + wv.shape[1:], BF16),
+            pltpu.VMEM((rows,) + vo.shape, BF16),
+            pltpu.VMEM(wd.shape, BF16),
+            pltpu.VMEM((rows,) + gain.shape, F32),
+            pltpu.VMEM((cols, rows) + text.shape, BF16),
+            pltpu.VMEM((hr, rows, count, PAD), BF16),
+            pltpu.VMEM((cols, tokens, depth), F32),
+            pltpu.SemaphoreType.DMA((sends,)),
+            pltpu.SemaphoreType.DMA((slots,)),
+            pltpu.SemaphoreType.DMA((8,)),
+        ],
+        compiler_params=pltpu.CompilerParams(
+            collective_id=0, has_side_effects=True, vmem_limit_bytes=56 << 20
+        ),
+        name="front",
+    )(*args)
 
 
 def dec_attn_kernel(low_ref, q_ref, start_ref, pos_ref, k_ref, v_ref, o_ref, *, scale):
@@ -210,54 +419,52 @@
     half_rows = text.shape[0] * C
     own_text = text.shape[0]
 
-    x_all = lax.all_gather(patches[0], ("col", "row"), axis=0)
-    x_all = x_all.reshape(C, R * patches.shape[1], patches.shape[2])
-    patch_total = x_all.shape[1]
+    dec_out_all = lax.all_gather(dec_out, ("col", "row"), axis=0)
+    dec_out_all = dec_out_all.reshape(C, R, hc, HEAD_DIM, dec_out.shape[1])
+    patch_total = R * patches.shape[1]
     head_of = c * hr // C
-    small = lax.all_gather(jnp.stack([vis_gain, vis_bias]), "col", axis=0)
-    wv = lax.all_gather(vis_qkv, "col", axis=0)
-    wv = lax.dynamic_slice_in_dim(wv, head_of * 3 * HEAD_DIM, 3 * HEAD_DIM, axis=2)
-    wv = pad_parts(wv)
-    wvb = pad_parts(lax.dynamic_slice_in_dim(vis_qkv_bias, head_of * 3 * HEAD_DIM, 3 * HEAD_DIM, 0))
-    text_all = lax.all_gather(text, ("col", "row"), axis=0).reshape(C, R, own_text, text.shape[1])
-    vis_out_all = lax.all_gather(vis_out, "row", axis=0, tiled=True)
+    small = jnp.pad(jnp.stack([vis_gain, vis_bias]).astype(F32), ((0, 6), (0, 0)))
+    wv = pad_parts(jnp.transpose(vis_qkv.reshape(-1, hr, 3 * HEAD_DIM), (1, 0, 2)))
+    wvb = lax.dynamic_slice_in_dim(vis_qkv_bias, head_of * 3 * HEAD_DIM, 3 * HEAD_DIM, 0)
+    wvb = pad_parts(wvb)[None]
+    vo = jnp.pad(vis_out.reshape(hr, HEAD_DIM, -1), ((0, 0), (0, PAD - HEAD_DIM), (0, 0)))
     wd = jnp.transpose(dec_qkv.reshape(dec_qkv.shape[0], hc, 3 * HEAD_DIM), (1, 0, 2))
     wd = pad_parts(jnp.repeat(wd, share, axis=0) if share > 1 else wd)
-    wd = lax.all_to_all(wd, "row", 0, 0)
-    dec_out_all = lax.all_gather(dec_out, ("col", "row"), axis=0)
-    dec_out_all = dec_out_all.reshape(C, R, hc, HEAD_DIM, dec_out.shape[1])
-    gain_all = lax.all_gather(dec_gain, "row", axis=0)[:, None]
-
-    patch_ids = segment_of(jnp.arange(patch_total, dtype=jnp.int32) // 4, image_lengths)
-    attn = vis_head(x_all, small[:, :1], small[:, 1:], wv, wvb[None], patch_ids, scale)
-    attn_all = lax.all_gather(attn[:, :HEAD_DIM], ("row", "col"), axis=0)
-    attn_all = attn_all.reshape(R, C, patch_total, HEAD_DIM)[:, :: C // hr]
-    attn_all = jnp.transpose(attn_all, (2, 0, 1, 3)).reshape(patch_total, HEADS * HEAD_DIM)
-    own_x = lax.dynamic_index_in_dim(x_all, c, 0, keepdims=False)
-    resid = (
-        own_x.astype(F32)
-        + jnp.dot(attn_all, vis_out_all, preferred_element_type=F32)
-        + vis_out_bias.astype(F32)
-    ).astype(BF16)
-    merged = resid.reshape(patch_total // 4, 4 * resid.shape[1])
-    partial = jnp.dot(
-        merged, proj_weight.reshape(4 * proj_weight.shape[1], -1), preferred_element_type=F32
+    gain = jnp.pad(dec_gain.astype(F32)[None], ((0, 7), (0, 0)))
+    images = image_tokens.shape[1]
+    meta = jnp.concatenate([image_lengths, gaps])
+    meta = jnp.pad(meta[None], ((0, 7), (0, PAD - meta.shape[0])))
+    patch = patches[0].reshape(-1, 4, patches.shape[2])
+    patch = jnp.transpose(patch, (1, 0, 2)).reshape(patches.shape[1:])
+    patch_ids = segment_of(jnp.arange(patch_total // 4, dtype=jnp.int32), image_lengths)
+    patch_ids = jnp.tile(patch_ids.reshape(R, 1, -1), (1, 4, 1)).reshape(patch_total)
+    qkv_text, qkv_image, image_all, meta = front(
+        patch, small, wv, wvb, patch_ids, vo, vis_out_bias[None], proj_weight,
+        proj_bias[None], text, gain, wd, meta, R, C, scale,
     )
-    image_rows = (lax.psum(partial, "col") + proj_bias.astype(F32)).astype(BF16)
-    image_all = lax.all_gather(image_rows, "row", axis=0)
-
-    text_qkv = dec_rows(text_all, gain_all, wd, TPD).reshape(half_rows, 3 * PAD)
-    image_qkv = dec_rows(image_all[None], gain_all, wd, image_rows.shape[0])[0]
-    source, inside = insert_map(jnp.arange(half_rows, dtype=jnp.int32), image_lengths, gaps)
-    pick = jnp.where(inside, source, -1)
-    hot = (pick[:, None] == jnp.arange(image_rows.shape[0], dtype=jnp.int32)[None]).astype(BF16)
-    placed = jnp.dot(hot, image_qkv, preferred_element_type=F32).astype(BF16)
-    qkv = jnp.where(inside[:, None], placed, text_qkv)
-    both = lax.all_gather(qkv[:, PAD:], "grp", axis=0)
+    image_rows = lax.dynamic_index_in_dim(image_all, r, 0, keepdims=False)
+
     t = jnp.arange(half_rows, dtype=jnp.int32)
+
+    def hot_of(lengths, spaces):
+        source, inside = insert_map(t, lengths, spaces)
+        pick = jnp.where(inside, source, -1)
+        hot = pick[:, None] == jnp.arange(image_rows.shape[0], dtype=jnp.int32)[None]
+        return hot.astype(BF16), inside
+
+    hot, inside = hot_of(image_lengths, gaps)
+    merged = []
+    for half in range(2):
+        hot_half, inside_half = hot_of(
+            meta[half, 0, :images], meta[half, 0, images : 2 * images + 1]
+        )
+        placed = jnp.dot(hot_half, qkv_image[half], preferred_element_type=F32).astype(BF16)
+        merged.append(jnp.where(inside_half[:, None], placed, qkv_text[half]))
+    both = jnp.stack(merged)
+    query = lax.dynamic_index_in_dim(both, g, 0, keepdims=False)[:, :PAD]
     at = t // TPD * (2 * TPD) + g * TPD + t % TPD
     begin = starts_of(at, doc_lengths)
-    out = dec_attn(qkv[:, :PAD], both[..., :PAD], both[..., PAD:], begin, at, scale)
+    out = dec_attn(query, both[..., PAD : 2 * PAD], both[..., 2 * PAD :], begin, at, scale)
 
     mine = half_rows // (C * R)
     spread = out[:, :HEAD_DIM].reshape(C * R, mine, HEAD_DIM)

time: 408 us -> 374 us (0.917)
  Pallas kernels: 25.4 us -> 288 us
  waiting for transfers between devices: 220 us -> 13.1 us
  blocking collectives: 71.3 us -> 0 us
  local copies, waits for them, and re-layouts: 45.3 us -> 29.5 us
  starting transfers between devices: 13 us -> 8.2 us
    pallas_call x3 -> x1, Pallas kernels: 13.6 us -> 276 us  [front(): pl.pallas_call(functools.partial(front_kernel, rows=rows, cols=cols, hr=h...]
    all_gather x6 -> x0, waiting for transfers between devices: 168 us -> none  [the longest x1 47.8 us: per_device(): vis_out_all = lax.all_gather(vis_out, 'row', axis=0, tiled=True)]
    all_gather x2 -> x0, blocking collectives: 41 us -> none  [the longest x1 39.1 us: per_device(): image_all = lax.all_gather(image_rows, 'row', axis=0)]
    all_gather x1, waiting for transfers between devices: 37.4 us -> 0.01 us  [per_device(): dec_out_all = lax.all_gather(dec_out, ('col', 'row'), axis=0)]
    unnamed x1 -> x0, blocking collectives: 30.3 us -> none
    all_gather x2 -> x0, local copies, waits for them, and re-layouts: 11.1 us -> none  [the longest x1 10.9 us: per_device(): lax.all_gather(text, ('col', 'row'), axis=0)]
    reshape x3 -> x0, local copies, waits for them, and re-layouts: 6.88 us -> none  [the longest x1 2.98 us: per_device(): attn_all = attn_all.reshape(R, C, patch_total, HEAD_DIM)[:, ::C // hr]]
  transfers between devices with their start and end apart: 11 -> 3, of which waited for: 8 -> 2; matrix products, arithmetic and copies ran while one was open for 8% -> 11% of each run, Pallas kernels for 3% -> 77%
where the time goes in v2:
time: 374 us; the launch traced here: 372 us
  Pallas kernels  288 us (77%)
  local copies, waits for them, and re-layouts  29.5 us (8%)
  between operations  13.8 us (4%)
  waiting for transfers between devices  13.1 us (4%)
  matrix products  12.8 us (3%)
  starting transfers between devices  8.2 us (2%)
  other arithmetic  6.87 us (2%)
    pallas_call x1, Pallas kernels, front(): pl.pallas_call(functools.partial(front_kernel, rows=rows, cols=cols, hr=h...  276 us
    pallas_call x1, Pallas kernels, dec_attn(): pl.pallas_call(functools.partial(dec_attn_kernel, scale=scale), grid_spec...  11.8 us
    all_to_all x1, waiting for transfers between devices, per_device(): delta = lax.all_to_all(delta, 'row', 0, 0).reshape(own_text, text.shape[1])  11 us
    reshape x1, local copies, waits for them, and re-layouts, per_device(): dec_out_all = dec_out_all.reshape(C, R, hc, HEAD_DIM, dec_out.shape[1])  10.8 us
  transfers between devices with their start and end apart: 3, of which 2 were waited for; matrix products, arithmetic and copies ran while one was open for 11% of the time, Pallas kernels for 77%

profile of v2, /device:TPU:0, one launch (start us, length us, event | category | flops | bytes accessed | tf_op | source)
XLA Modules:
  0.0 371.9 jit_solution(14170471471286456065)
XLA Ops:
  6.5 0.7 all-gather.4.cloned.1.call-update
  7.3 0.8 reduce-window.43
  8.3 0.9 tile.15.ids_ref
  9.2 0.7 tile.14.idk_ref
  9.8 0.8 dynamic_slice.19
  10.7 0.6 copy.79
  11.3 2.0 copy.53
  13.3 1.1 copy.54
  14.3 0.3 pad.39
  14.6 1.5 copy.68.wd_in
  16.2 1.4 copy.56.wv_in
  17.7 1.5 copy.58.proj_ref
  19.2 0.8 pad.36.vo_in
  20.0 0.7 copy.52
  20.8 0.6 pad.40.meta_in
  21.4 0.6 broadcast_in_dim.60.vob_ref
  22.0 0.5 broadcast_in_dim.61.projb_ref
  22.6 0.6 pad_convert_fusion.gain_in
  23.2 0.6 fusion.53.small_ref
  23.8 275.9 %front.1 = (bf16[2,2048,384]{2,1,0:T(8,128)(2,1)}, bf16[2,128,384]{2,1,0:T(8,128)(2,1)}, bf16[8,128,176]{2,1,0:T(8,128)(2,1)}, s32[2,8,128]{2,1,0:T(8,128)}) custom-call(bf16[64,704]{1,0:T(8,128)(2,1)} %bitcast.139, f32[8,704]{1,0:T(8,128)} %fusion.53.small_ref, bf16[2,704,384]{2,1,0:T(8,128)(2,1)} %copy.56.wv_in, bf16[1,384]{1,0:T(2,128)(2,1)} %bitcast.144, ...), custom_call_target="tpu_custom_call" | custom-call | tf_op jit(solution)/shard_map/front/pallas_call | solution.py:292
  299.7 0.8 slice_bitcast_fusion
  300.4 0.2 reduce-window.45
  300.6 0.7 slice_bitcast_fusion.2
  301.3 0.2 reduce-window.46
  301.5 0.2 reduce-window.47
  301.7 0.2 reduce-window.48
  301.8 0.7 bitcast_add_fusion
  302.5 0.1 fusion.43
  302.8 3.7 fusion.5
  306.5 2.3 fusion.3
  308.9 0.7 fusion.11
  309.5 0.5 copy-done
  310.0 0.2 reduce-window.44
  310.4 0.4 copy.60.start_ref
  310.8 0.2 fusion.28.pos_ref
  311.0 1.4 pad_maximum_fusion
  312.5 11.8 %dec_attn.1 = bf16[2048,128]{1,0:T(8,128)(2,1)S(1)} custom-call(s32[8]{0:T(128)S(1)} %and_select_fusion.low_ref, bf16[2048,128]{1,0:T(8,128)(2,1)S(1)} %slice.76.q_ref, s32[2048,1]{1,0:T(8,128)S(1)} %copy.60.start_ref, s32[2048,1]{1,0:T(8,128)S(1)} %fusion.28.pos_ref, bf16[2,2048,128]{2,1,0:T(8,128)(2,1)S(1)} %get-tuple-element.20.k_ref, ...), custom_call_target="tpu_custom_call" | custom-call | tf_op jit(solution)/shard_map/dec_attn/pallas_call | solution.py:362
  324.3 0.9 copy.61
  325.2 3.5 all-to-all-start
  328.8 0.2 reduce-window.42
  329.0 10.8 %reshape.304 = bf16[2,8,8,88,176]{3,2,4,1,0:T(8,128)(2,1)} reshape(bf16[16,704,176]{1,2,0:T(8,128)(2,1)} %all-gather.4.cloned.1.call-done) | data formatting | bytes 7929856 | tf_op jit(solution)/shard_map/reshape | solution.py:423
  339.8 1.3 all-to-all-done
  341.1 5.6 %fusion.21 = bf16[8,128,176]{1,2,0:T(8,128)(2,1)} fusion(bf16[2,8,128,88,1]{2,3,1,4,0:T(8,128)(2,1)S(1)} %bitcast.140, bf16[2,8,8,88,176]{3,2,4,1,0:T(8,128)(2,1)} %reshape.304), kind=kOutput, calls=%fused_computation.28 | convolution fusion | flops 507691008 | bytes 4685824 | tf_op jit(solution)/shard_map/chte,crhef->rtf/dot_general | solution.py:473
  346.7 4.6 %all-to-all-start.1 = ((bf16[8,128,176]{1,2,0:T(8,128)(2,1)}), bf16[8,128,176]{1,2,0:T(8,128)(2,1)S(1)}, u32[]{:S(2)}, u32[]{:S(2)}) async-start(bf16[8,128,176]{1,2,0:T(8,128)(2,1)} %fusion.21), calls=%async_computation.1 | async-start | bytes 720896 | tf_op jit(solution)/shard_map/all_to_all | solution.py:476
  351.6 11.0 %all-to-all-done.1 = bf16[8,128,176]{1,2,0:T(8,128)(2,1)S(1)} async-done(((bf16[8,128,176]{1,2,0:T(8,128)(2,1)}), bf16[8,128,176]{1,2,0:T(8,128)(2,1)S(1)}, u32[]{:S(2)}, u32[]{:S(2)}) %all-to-all-start.1) | async-done | bytes 360480 | tf_op jit(solution)/shard_map/all_to_all | solution.py:476
  362.7 0.2 copy.63
  362.9 1.2 fusion.20
  364.1 0.9 copy.64
  (60 shorter events, 1.2 us)
Async XLA Ops:
  6.5 6.7 %copy-start.4 = (bf16[176,2112]{1,0:T(8,128)(2,1)S(1)}, bf16[176,2112]{1,0:T(8,128)(2,1)}, u32[]{:S(2)}) copy-start(bf16[176,2112]{1,0:T(8,128)(2,1)} %param.27) | copy-start | bytes 2230276
  6.5 322.4 %all-gather.4.cloned.1.call-start = ((), (), s32[]{:S(2)}) async-start(), calls=%async_computation.2 | async-start | bytes 4595712 | tf_op jit(solution)/shard_map/all_gather | solution.py:422
  14.6 1.5 copy-start.3
  16.2 1.4 copy-start.2
  17.6 1.6 copy-start.5
  17.6 2.4 copy-start.6
  17.6 3.1 copy-start.7
  17.6 3.1 copy-start.8
  17.6 3.1 copy-start.14
  17.6 3.1 copy-start.11
  17.6 3.1 copy-start.16
  17.7 3.8 %copy-start.9 = (bf16[704]{0:T(1024)(128)(2,1)S(1)}, bf16[704]{0:T(1024)(128)(2,1)}, u32[]{:S(2)}) copy-start(bf16[704]{0:T(1024)(128)(2,1)} %param.22) | copy-start | bytes 4228
  17.7 4.4 %copy-start.15 = (bf16[176]{0:T(256)(128)(2,1)S(1)}, bf16[176]{0:T(256)(128)(2,1)}, u32[]{:S(2)}) copy-start(bf16[176]{0:T(256)(128)(2,1)} %param.24) | copy-start | bytes 1060
  302.8 3.7 copy-start.12
  302.8 3.7 copy-start.13
  308.8 1.2 copy-start
  308.8 1.2 copy-start.10
  325.2 15.9 %all-to-all-start = ((bf16[16,128,88]{1,2,0:T(8,128)(2,1)}), bf16[16,128,88]{1,2,0:T(8,128)(2,1)S(1)}, u32[]{:S(2)}, u32[]{:S(2)}) async-start(bf16[16,128,88]{1,2,0:T(8,128)(2,1)} %copy.61), calls=%async_computation | async-start | bytes 720896 | tf_op jit(solution)/shard_map/all_to_all | solution.py:471
  346.7 16.2 %copy-start.1 = (bf16[1,1024,176]{2,1,0:T(8,128)(2,1)S(1)}, bf16[1,1024,176]{2,1,0:T(8,128)(2,1)}, u32[]{:S(2)}) copy-start(bf16[1,1024,176]{2,1,0:T(8,128)(2,1)} %copy.53) | copy-start | bytes 1081348
  346.7 16.0 %all-to-all-start.1 = ((bf16[8,128,176]{1,2,0:T(8,128)(2,1)}), bf16[8,128,176]{1,2,0:T(8,128)(2,1)S(1)}, u32[]{:S(2)}, u32[]{:S(2)}) async-start(bf16[8,128,176]{1,2,0:T(8,128)(2,1)} %fusion.21), calls=%async_computation.1 | async-start | bytes 720896 | tf_op jit(solution)/shard_map/all_to_all | solution.py:476
Sparse Core Ops, SparseCore 0:
  9.6 82.1 all-gather.3

commit v3 on v2

--- a/solution.py
+++ b/solution.py
@@ -113,14 +113,20 @@
 
 def front_kernel(
     patch_ref, small_ref, wv_in, wvb_ref, ids_ref, idk_ref, vo_in, vob_ref, proj_ref, projb_ref,
-    text_in, gain_in, wd_in, meta_in,
-    qkv_ref, img_ref, image_ref, meta_ref,
-    x_ref, s_ref, wv_ref, vo_ref, wd_ref, gain_ref, text_ref, at_ref, part_ref,
-    send, recv, local,
-    *, rows, cols, hr, scale, width,
+    gain_in, wd_in, meta_in, *rest,
+    texts, rows, cols, hr, scale, width,
 ):
+    text_in, rest = rest[:texts], rest[texts:]
+    (q_ref, kv_ref, imgq_ref, imgkv_ref, image_ref, meta_ref, x_ref, s_ref, wv_ref, vo_ref, wd_ref,
+     gain_ref, at_ref, part_ref, send, recv, local), text_ref = rest[:17], rest[17:]
     net = Links(send, recv, rows, cols)
     r, c, g = net.r, net.c, net.g
+    k_out = vo_in.shape[1] // 2
+    k_dec = wd_in.shape[1] // 2
+    vo_half = pl.ds(pl.multiple_of(g * k_out, 16), k_out)
+    vo_rest = pl.ds(pl.multiple_of((1 - g) * k_out, 16), k_out)
+    wd_half = pl.ds(pl.multiple_of(g * k_dec, 16), k_dec)
+    wd_rest = pl.ds(pl.multiple_of((1 - g) * k_dec, 16), k_dec)
     barrier = pltpu.get_barrier_semaphore()
     for step in range(1, rows):
         pl.semaphore_signal(barrier, inc=1, device_id={"row": (r + step) % rows},
@@ -136,12 +142,12 @@
         (patch_ref, x_ref.at[c, r]),
         (small_ref, s_ref.at[c]),
         (wv_in.at[c * hr // cols], wv_ref.at[c]),
-        (vo_in, vo_ref.at[r]),
-        (wd_in.at[r], wd_ref.at[r]),
+        (vo_in.at[:, vo_half], vo_ref.at[r, :, vo_half]),
+        (wd_in.at[r, wd_half], wd_ref.at[r, wd_half]),
         (gain_in, gain_ref.at[r]),
-        (text_in, text_ref.at[c, r]),
         (meta_in, meta_ref.at[g]),
     ]
+    own += [(a, b.at[c, r]) for a, b in zip(text_in, text_ref)]
     own = [pltpu.make_async_copy(a, b, local.at[i]) for i, (a, b) in enumerate(own)]
     for copy in own:
         copy.start()
@@ -149,10 +155,12 @@
     x_row, x_col = net.slots(rows), net.slots(cols)
     s_col, wv_col = net.slots(cols), net.slots(cols)
     vo_row, wd_row, gain_row = net.slots(rows), net.slots(rows), net.slots(rows)
-    text_row, text_col = net.slots(rows), net.slots(cols)
+    text_row = [net.slots(rows) for _ in text_in]
+    text_col = [net.slots(cols) for _ in text_in]
     at_row, at_col = net.slots(rows), net.slots(cols)
     part_col, img_row, meta_grp = net.slots(cols), net.slots(rows), net.slots(1)
-    kv_grp, imgkv_grp = net.slots(1), net.slots(1)
+    kv_grp, imgkv_grp = net.slots(cols), net.slots(1)
+    vo_grp, wd_grp = net.slots(1), net.slots(1)
 
     net.row_start(patch_ref, x_ref.at[c], x_row)
     net.col_start(small_ref, s_ref.at[c], s_col)
@@ -161,11 +169,10 @@
         net.push(wv_in.at[to * hr // cols], wv_ref.at[c], wv_col + c, col=to)
     net.push(meta_in, meta_ref.at[g], meta_grp, grp=1 - g)
     net.row_start(gain_in, gain_ref, gain_row)
-    net.row_start(text_in, text_ref.at[c], text_row)
-    net.row_start(vo_in, vo_ref, vo_row)
+    net.row_start(vo_in.at[:, vo_half], vo_ref.at[:, :, vo_half], vo_row)
     for step in range(1, rows):
         to = (r + step) % rows
-        net.push(wd_in.at[to], wd_ref.at[r], wd_row + r, row=to)
+        net.push(wd_in.at[to, wd_half], wd_ref.at[r, wd_half], wd_row + r, row=to)
     for copy in own:
         copy.wait()
     net.row_forward(x_ref.at[c], x_row)
@@ -203,14 +210,21 @@
     mine = c * hr // cols
     at_ref[mine, r] = mixed.astype(BF16)
     net.row_start(at_ref.at[mine, r], at_ref.at[mine], at_row)
+    for a, b, base in zip(text_in, text_ref, text_row):
+        net.row_start(a, b.at[c], base)
+    net.row_forward(vo_ref.at[:, :, vo_half], vo_row)
+    net.row_finish(vo_ref.at[:, :, vo_half], vo_row)
+    net.push(vo_ref.at[:, :, vo_half], vo_ref.at[:, :, vo_half], vo_grp, grp=1 - g)
     net.row_forward(at_ref.at[mine], at_row)
-    net.row_forward(text_ref.at[c], text_row)
     net.row_finish(at_ref.at[mine], at_row)
     for step in range(1, hr):
         to = (c + step * (cols // hr)) % cols
         net.push(at_ref.at[mine], at_ref.at[mine], at_col + mine, col=to)
-    net.row_forward(vo_ref, vo_row)
-    net.row_finish(vo_ref, vo_row)
+    for step in range(1, rows):
+        at = (r + step) % rows
+        net.arrived(wd_ref.at[at, wd_half], wd_row + at)
+    net.push(wd_ref.at[:, wd_half], wd_ref.at[:, wd_half], wd_grp, grp=1 - g)
+    net.arrived(vo_ref.at[:, :, vo_rest], vo_grp)
     for step in range(1, hr):
         other = (mine + step) % hr
         net.arrived(at_ref.at[other], at_col + other)
@@ -218,7 +232,9 @@
     delta = x_ref[c].reshape(count, depth).astype(F32) + vob_ref[...].astype(F32)
     for i in range(rows):
         for h in range(hr):
-            delta += jnp.dot(at_ref[h, i], vo_ref[i, h], preferred_element_type=F32)
+            delta += jnp.dot(
+                at_ref[h, i][:, : 2 * k_out], vo_ref[i, h], preferred_element_type=F32
+            )
     tokens = count // 4
     resid = delta.astype(BF16).reshape(rows, 4, tokens // rows, depth)
     partial = jnp.zeros(part_ref.shape[1:], F32)
@@ -235,12 +251,13 @@
     net.row_start(image_ref.at[r], image_ref, img_row)
     net.row_forward(gain_ref, gain_row)
     net.row_finish(gain_ref, gain_row)
-    net.row_finish(text_ref.at[c], text_row)
-    net.col_start(text_ref.at[c], text_ref.at[c], text_col)
-    for step in range(1, rows):
-        at = (r + step) % rows
-        net.arrived(wd_ref.at[at], wd_row + at)
+    for b, base in zip(text_ref, text_row):
+        net.row_forward(b.at[c], base)
+    for b, base, other in zip(text_ref, text_row, text_col):
+        net.row_finish(b.at[c], base)
+        net.col_start(b.at[c], b.at[c], other)
     net.row_forward(image_ref, img_row)
+    net.arrived(wd_ref.at[:, wd_rest], wd_grp)
 
     def head_rows(part):
         number = part(0).shape[0]
@@ -255,49 +272,72 @@
             total += jnp.dot(normed, wd_ref[i], preferred_element_type=F32)
         return total.astype(BF16)
 
-    own_rows = text_in.shape[0]
+    own_rows = sum(b.shape[2] for b in text_ref[:2])
 
     def text_block(at):
-        @pl.loop(0, own_rows // TPD)
-        def _(j):
-            start = pl.multiple_of(j * TPD, TPD)
-            found = head_rows(lambda i: text_ref[at, i, pl.ds(start, TPD)])
-            qkv_ref[g, pl.ds(pl.multiple_of(at * own_rows + start, TPD), TPD)] = found
+        for piece in range(2):
+            @pl.loop(0, own_rows // 2 // TPD)
+            def _(j):
+                take = pl.ds(pl.multiple_of(j * TPD, TPD), TPD)
+
+                def part(i):
+                    x = text_ref[piece][at, i, take]
+                    if len(text_ref) < 3:
+                        return x
+                    tail = text_ref[2][at, i, take]
+                    return jnp.concatenate([x, tail[:, piece * 64 : piece * 64 + 64]], axis=1)
+
+                found = head_rows(part)
+                put = at * own_rows + piece * (own_rows // 2) + j * TPD
+                put = pl.ds(pl.multiple_of(put, TPD), TPD)
+                q_ref[put] = found[:, :PAD]
+                kv_ref[g, put] = found[:, PAD:]
+        rows_of = pl.ds(pl.multiple_of(at * own_rows, TPD), own_rows)
+        net.push(kv_ref.at[g, rows_of], kv_ref.at[g, rows_of], kv_grp + at, grp=1 - g)
 
     text_block(c)
     net.row_finish(image_ref, img_row)
-    img_ref[g] = head_rows(lambda i: image_ref[i])
-    net.push(img_ref.at[g], img_ref.at[g], imgkv_grp, grp=1 - g)
-    net.col_finish(text_ref, text_col)
+    found = head_rows(lambda i: image_ref[i])
+    imgq_ref[...] = found[:, :PAD]
+    imgkv_ref[g] = found[:, PAD:]
+    net.push(imgkv_ref.at[g], imgkv_ref.at[g], imgkv_grp, grp=1 - g)
+    for b, base in zip(text_ref, text_col):
+        net.col_finish(b, base)
     for step in range(1, cols):
         text_block((c + step) % cols)
-    net.push(qkv_ref.at[g], qkv_ref.at[g], kv_grp, grp=1 - g)
     net.arrived(meta_ref.at[1 - g], meta_grp)
-    net.arrived(img_ref.at[1 - g], imgkv_grp)
-    net.arrived(qkv_ref.at[1 - g], kv_grp)
+    net.arrived(imgkv_ref.at[1 - g], imgkv_grp)
+    for step in range(cols):
+        at = (c + step) % cols
+        rows_of = pl.ds(pl.multiple_of(at * own_rows, TPD), own_rows)
+        net.arrived(kv_ref.at[1 - g, rows_of], kv_grp + at)
     for copy in net.pending:
         copy.wait_send()
 
 
-def front(patch, small, wv, wvb, ids, vo, vob, proj, projb, text, gain, wd, meta, rows, cols, scale):
+def front(patch, small, wv, wvb, ids, vo, vob, proj, projb, texts, gain, wd, meta, rows, cols, scale):
     hr = wv.shape[0]
     count = rows * patch.shape[0]
-    half = cols * text.shape[0]
+    half = cols * 2 * texts[0].shape[0]
+    number = len(texts)
     tokens = count // 4
     depth = proj.shape[2]
-    args = (patch, small, wv, wvb, ids[:, None], ids[None, :], vo, vob, proj, projb, text, gain, wd, meta)
-    sends = 6 * (rows - 1) + (rows - 1) + 6 * (cols - 1) + 3
-    slots = 7 * rows + 6 * cols + 3
+    args = (patch, small, wv, wvb, ids[:, None], ids[None, :], vo, vob, proj, projb, gain, wd, meta) + tuple(texts)
+    sends = (6 + number) * (rows - 1) + (5 + number) * (cols - 1) + 4 + cols
+    slots = (6 + number) * rows + (5 + number) * cols + 4 + cols
     vmem = pl.BlockSpec(memory_space=pltpu.VMEM)
     return pl.pallas_call(
         functools.partial(
-            front_kernel, rows=rows, cols=cols, hr=hr, scale=scale, width=HEADS * HEAD_DIM
+            front_kernel, texts=number, rows=rows, cols=cols, hr=hr, scale=scale,
+            width=HEADS * HEAD_DIM,
         ),
         in_specs=[vmem] * len(args),
-        out_specs=[vmem] * 4,
+        out_specs=[vmem] * 6,
         out_shape=[
-            jax.ShapeDtypeStruct((2, half, 3 * PAD), BF16),
-            jax.ShapeDtypeStruct((2, tokens, 3 * PAD), BF16),
+            jax.ShapeDtypeStruct((half, PAD), BF16),
+            jax.ShapeDtypeStruct((2, half, 2 * PAD), BF16),
+            jax.ShapeDtypeStruct((tokens, PAD), BF16),
+            jax.ShapeDtypeStruct((2, tokens, 2 * PAD), BF16),
             jax.ShapeDtypeStruct((rows, tokens, depth), BF16),
             jax.ShapeDtypeStruct((2,) + meta.shape, jnp.int32),
         ],
@@ -308,13 +348,13 @@
             pltpu.VMEM((rows,) + vo.shape, BF16),
             pltpu.VMEM(wd.shape, BF16),
             pltpu.VMEM((rows,) + gain.shape, F32),
-            pltpu.VMEM((cols, rows) + text.shape, BF16),
             pltpu.VMEM((hr, rows, count, PAD), BF16),
             pltpu.VMEM((cols, tokens, depth), F32),
             pltpu.SemaphoreType.DMA((sends,)),
             pltpu.SemaphoreType.DMA((slots,)),
-            pltpu.SemaphoreType.DMA((8,)),
-        ],
+            pltpu.SemaphoreType.DMA((7 + number,)),
+        ]
+        + [pltpu.VMEM((cols, rows) + text.shape, BF16) for text in texts],
         compiler_params=pltpu.CompilerParams(
             collective_id=0, has_side_effects=True, vmem_limit_bytes=56 << 20
         ),
@@ -420,17 +460,31 @@
     own_text = text.shape[0]
 
     dec_out_all = lax.all_gather(dec_out, ("col", "row"), axis=0)
-    dec_out_all = dec_out_all.reshape(C, R, hc, HEAD_DIM, dec_out.shape[1])
+    dec_out_all = dec_out_all.reshape((C, R) + dec_out.shape)
     patch_total = R * patches.shape[1]
     head_of = c * hr // C
     small = jnp.pad(jnp.stack([vis_gain, vis_bias]).astype(F32), ((0, 6), (0, 0)))
     wv = pad_parts(jnp.transpose(vis_qkv.reshape(-1, hr, 3 * HEAD_DIM), (1, 0, 2)))
     wvb = lax.dynamic_slice_in_dim(vis_qkv_bias, head_of * 3 * HEAD_DIM, 3 * HEAD_DIM, 0)
     wvb = pad_parts(wvb)[None]
-    vo = jnp.pad(vis_out.reshape(hr, HEAD_DIM, -1), ((0, 0), (0, PAD - HEAD_DIM), (0, 0)))
+    vo = jnp.pad(vis_out.reshape(hr, HEAD_DIM, -1), ((0, 0), (0, 96 - HEAD_DIM), (0, 0)))
     wd = jnp.transpose(dec_qkv.reshape(dec_qkv.shape[0], hc, 3 * HEAD_DIM), (1, 0, 2))
     wd = pad_parts(jnp.repeat(wd, share, axis=0) if share > 1 else wd)
-    gain = jnp.pad(dec_gain.astype(F32)[None], ((0, 7), (0, 0)))
+    depth = text.shape[1]
+    split = own_text // 2
+    wide = PAD if depth <= PAD else PAD + 64
+    more = wide - depth
+    wd = jnp.pad(wd, ((0, 0), (0, more), (0, 0)))
+    gain = jnp.pad(dec_gain.astype(F32)[None], ((0, 7), (0, more)))
+    proj = jnp.pad(proj_weight, ((0, 0), (0, 0), (0, more)))
+    projb = jnp.pad(proj_bias, (0, more))
+    if depth <= PAD:
+        filled = jnp.pad(text, ((0, 0), (0, more)))
+        texts = [filled[:split], filled[split:]]
+    else:
+        tail = jnp.pad(text[:, PAD:], ((0, 0), (0, more)))
+        texts = [text[:split, :PAD], text[split:, :PAD]]
+        texts.append(jnp.concatenate([tail[:split], tail[split:]], axis=1))
     images = image_tokens.shape[1]
     meta = jnp.concatenate([image_lengths, gaps])
     meta = jnp.pad(meta[None], ((0, 7), (0, PAD - meta.shape[0])))
@@ -438,11 +492,11 @@
     patch = jnp.transpose(patch, (1, 0, 2)).reshape(patches.shape[1:])
     patch_ids = segment_of(jnp.arange(patch_total // 4, dtype=jnp.int32), image_lengths)
     patch_ids = jnp.tile(patch_ids.reshape(R, 1, -1), (1, 4, 1)).reshape(patch_total)
-    qkv_text, qkv_image, image_all, meta = front(
-        patch, small, wv, wvb, patch_ids, vo, vis_out_bias[None], proj_weight,
-        proj_bias[None], text, gain, wd, meta, R, C, scale,
+    q_text, kv_text, q_image, kv_image, image_all, meta = front(
+        patch, small, wv, wvb, patch_ids, vo, vis_out_bias[None], proj,
+        projb[None], texts, gain, wd, meta, R, C, scale,
     )
-    image_rows = lax.dynamic_index_in_dim(image_all, r, 0, keepdims=False)
+    image_rows = lax.dynamic_index_in_dim(image_all, r, 0, keepdims=False)[:, :depth]
 
     t = jnp.arange(half_rows, dtype=jnp.int32)
 
@@ -458,20 +512,22 @@
         hot_half, inside_half = hot_of(
             meta[half, 0, :images], meta[half, 0, images : 2 * images + 1]
         )
-        placed = jnp.dot(hot_half, qkv_image[half], preferred_element_type=F32).astype(BF16)
-        merged.append(jnp.where(inside_half[:, None], placed, qkv_text[half]))
+        placed = jnp.dot(hot_half, kv_image[half], preferred_element_type=F32).astype(BF16)
+        merged.append(jnp.where(inside_half[:, None], placed, kv_text[half]))
     both = jnp.stack(merged)
-    query = lax.dynamic_index_in_dim(both, g, 0, keepdims=False)[:, :PAD]
+    placed = jnp.dot(hot, q_image, preferred_element_type=F32).astype(BF16)
+    query = jnp.where(inside[:, None], placed, q_text)
     at = t // TPD * (2 * TPD) + g * TPD + t % TPD
     begin = starts_of(at, doc_lengths)
-    out = dec_attn(query, both[..., PAD : 2 * PAD], both[..., 2 * PAD :], begin, at, scale)
+    out = dec_attn(query, both[..., :PAD], both[..., PAD:], begin, at, scale)
 
     mine = half_rows // (C * R)
     spread = out[:, :HEAD_DIM].reshape(C * R, mine, HEAD_DIM)
     rows = lax.all_to_all(spread, ("col", "row"), 0, 0)
     rows = rows.reshape(C, R, mine, HEAD_DIM)[:, ::share]
+    rows = jnp.transpose(rows, (0, 2, 1, 3)).reshape(C, mine, hc * HEAD_DIM)
     delta = jnp.einsum(
-        "chte,crhef->rtf", rows, dec_out_all, preferred_element_type=F32
+        "ctk,crkf->rtf", rows, dec_out_all, preferred_element_type=F32
     ).astype(BF16)
     delta = lax.all_to_all(delta, "row", 0, 0).reshape(own_text, text.shape[1])
     own_hot = lax.dynamic_slice_in_dim(hot, c * own_text, own_text, 0)

time: 374 us -> 264 us (0.71)
  Pallas kernels: 288 us -> 179 us
  blocking collectives: 0 us -> 18.3 us
  local copies, waits for them, and re-layouts: 29.5 us -> 19.7 us
  starting transfers between devices: 8.2 us -> 3.45 us
    pallas_call x1, Pallas kernels: 276 us -> 166 us  [front(): pl.pallas_call(functools.partial(front_kernel, texts=number, rows=rows, c...]
    all_to_all x0 -> x1, blocking collectives: none -> 18.3 us  [per_device(): rows = lax.all_to_all(spread, ('col', 'row'), 0, 0)]
    reshape x1 -> x0, local copies, waits for them, and re-layouts: 10.8 us -> none  [per_device(): dec_out_all = dec_out_all.reshape(C, R, hc, HEAD_DIM, dec_out.shape[1])]
    dot_general x3 -> x4, matrix products: 11.5 us -> 11.5 us  [the longest x2 5.31 us: per_device(): jnp.dot(hot_half, kv_image[half], preferred_element_type=F32).astype(BF16)]
  transfers between devices with their start and end apart: 3 -> 2, of which waited for: 2 -> 1; matrix products, arithmetic and copies ran while one was open for 11% -> 12% of each run, Pallas kernels for 77% -> 68%
where the time goes in v3:
time: 264 us; the launch traced here: 263 us
  Pallas kernels  179 us (68%)
  local copies, waits for them, and re-layouts  19.7 us (7%)
  blocking collectives  18.3 us (7%)
  between operations  13.8 us (5%)
  matrix products  11.8 us (4%)
  waiting for transfers between devices  9.98 us (4%)
  other arithmetic  6.6 us (2%)
  starting transfers between devices  3.45 us (1%)
    pallas_call x1, Pallas kernels, front(): pl.pallas_call(functools.partial(front_kernel, texts=number, rows=rows, c...  166 us
    all_to_all x1, blocking collectives, per_device(): rows = lax.all_to_all(spread, ('col', 'row'), 0, 0)  18.3 us
    pallas_call x1, Pallas kernels, dec_attn(): pl.pallas_call(functools.partial(dec_attn_kernel, scale=scale), grid_spec...  13.6 us
    all_to_all x1, waiting for transfers between devices, per_device(): delta = lax.all_to_all(delta, 'row', 0, 0).reshape(own_text, text.shape[1])  9.27 us
    dot_general x2, matrix products, per_device(): jnp.dot(hot_half, kv_image[half], preferred_element_type=F32).astype(BF16)  5.31 us
  transfers between devices with their start and end apart: 2, of which 1 were waited for; matrix products, arithmetic and copies ran while one was open for 12% of the time, Pallas kernels for 68%

profile of v3, /device:TPU:0, one launch (start us, length us, event | category | flops | bytes accessed | tf_op | source)
XLA Modules:
  0.0 262.8 jit_solution(9901051734582886458)
XLA Ops:
  6.5 0.7 all-gather.4.cloned.1.call-update
  7.3 0.8 reduce-window.43
  8.3 0.9 tile.15.ids_ref
  9.2 0.7 tile.14.idk_ref
  9.8 0.8 dynamic_slice.15
  10.7 0.5 copy.70
  11.2 1.2 copy.56
  12.5 1.1 copy.54
  13.6 0.2 pad.57
  13.8 0.8 copy.67
  14.6 1.3 pad.58.wd_in
  15.9 1.7 copy.53
  17.6 1.3 pad.53.proj_ref
  19.1 1.4 copy.57.wv_in
  20.5 0.7 pad.52.vo_in
  21.3 0.6 copy.52
  22.1 0.6 pad.59.meta_in
  22.7 0.6 broadcast_in_dim.68.vob_ref
  23.3 0.6 broadcast_in_dim.72.projb_ref
  23.9 0.6 pad_convert_fusion.gain_in
  24.5 0.6 fusion.42.small_ref
  25.1 0.8 fusion.52
  25.9 165.7 %front.1 = (bf16[2048,128]{1,0:T(8,128)(2,1)}, bf16[2,2048,256]{2,1,0:T(8,128)(2,1)}, bf16[128,128]{1,0:T(8,128)(2,1)}, bf16[2,128,256]{2,1,0:T(8,128)(2,1)}, bf...) custom-call(bf16[64,704]{1,0:T(8,128)(2,1)} %bitcast.143, f32[8,704]{1,0:T(8,128)} %fusion.42.small_ref, ...), custom_call_target="tpu_custom_call" | custom-call | tf_op jit(solution)/shard_map/front/pallas_call | solution.py:329
  191.6 0.8 slice_bitcast_fusion
  192.4 0.2 reduce-window.45
  192.6 0.7 slice_bitcast_fusion.2
  193.3 0.2 reduce-window.46
  193.5 0.2 reduce-window.47
  193.6 0.2 reduce-window.48
  193.8 0.2 reduce-window.42
  194.4 0.4 copy.60.start_ref
  194.8 0.8 bitcast_add_fusion
  196.3 3.3 %fusion.1 = bf16[1,2048,256]{2,1,0:T(8,128)(2,1)S(1)} fusion(bf16[2,2048,256]{2,1,0:T(8,128)(2,1)} %get-tuple-element.16, pred[2048]{0:T(1024)(128)(4,1)S(1)} %fusion.33, s32[2048]{0:T(1024)S(1)} %broadcast_select_fusion.1, bf16[2,128,256]{2,1,0:T(8,128)(2,1)} %get-tuple-element.15), kind=kOutput, calls=%fused_computation.3 | convolution fusion | flops 135528448 | bytes 2172928 | tf_op jit(solution)/shard_map/dot_general | solution.py:515
  199.6 2.0 fusion.3
  201.7 0.2 fusion.18.pos_ref
  201.9 2.0 fusion.4.q_ref
  203.9 0.4 pad_maximum_fusion
  204.3 13.6 %dec_attn.1 = bf16[2048,128]{1,0:T(8,128)(2,1)S(1)} custom-call(s32[8]{0:T(128)S(1)} %and_select_fusion.low_ref, bf16[2048,128]{1,0:T(8,128)(2,1)S(1)} %fusion.4.q_ref, s32[2048,1]{1,0:T(8,128)S(1)} %copy.60.start_ref, s32[2048,1]{1,0:T(8,128)S(1)} %fusion.18.pos_ref, bf16[2,2048,128]{2,1,0:T(8,128)(2,1)S(1)} %get-tuple-element.24.k_ref, ...), custom_call_target="tpu_custom_call" | custom-call | tf_op jit(solution)/shard_map/dec_attn/pallas_call | solution.py:402
  217.9 0.2 copy.61
  218.1 18.3 %all_to_all.10 = bf16[16,128,88]{1,2,0:T(8,128)(2,1)S(1)} all-to-all(bf16[16,128,88]{1,2,0:T(8,128)(2,1)S(1)} %copy.61), channel_id=1, replica_groups=mesh['row'=8,'col'=2,'grp'=2] {'col','row'}, dimensions={0} | all-to-all | bytes 720896 | tf_op jit(solution)/shard_map/all_to_all | solution.py:526
  236.4 4.2 %fusion.13 = bf16[8,128,176]{1,2,0:T(8,128)(2,1)} fusion(bf16[2,128,704,1]{1,2,3,0:T(8,128)(2,1)S(1)} %bitcast.144, bf16[2,8,704,176]{2,3,1,0:T(8,128)(2,1)} %bitcast.154), kind=kOutput, calls=%fused_computation.24 | convolution fusion | flops 507691008 | bytes 4685824 | tf_op jit(solution)/shard_map/ctk,crkf->rtf/dot_general | solution.py:529
  240.6 3.4 %all-to-all-start.1 = ((bf16[8,128,176]{1,2,0:T(8,128)(2,1)}), bf16[8,128,176]{1,2,0:T(8,128)(2,1)S(1)}, u32[]{:S(2)}, u32[]{:S(2)}) async-start(bf16[8,128,176]{1,2,0:T(8,128)(2,1)} %fusion.13), calls=%async_computation.1 | async-start | bytes 720896 | tf_op jit(solution)/shard_map/all_to_all | solution.py:532
  244.1 0.9 dynamic-slice_bitcast_fusion
  244.9 0.3 iota_compare_fusion.2
  245.3 9.3 %all-to-all-done.1 = bf16[8,128,176]{1,2,0:T(8,128)(2,1)S(1)} async-done(((bf16[8,128,176]{1,2,0:T(8,128)(2,1)}), bf16[8,128,176]{1,2,0:T(8,128)(2,1)S(1)}, u32[]{:S(2)}, u32[]{:S(2)}) %all-to-all-start.1) | async-done | bytes 360480 | tf_op jit(solution)/shard_map/all_to_all | solution.py:532
  254.5 0.2 copy.63
  254.8 0.3 fusion.12
  255.1 0.9 copy.64
  (64 shorter events, 1.7 us)
Async XLA Ops:
  6.5 5.9 %copy-start.1 = (bf16[176,2112]{1,0:T(8,128)(2,1)S(1)}, bf16[176,2112]{1,0:T(8,128)(2,1)}, u32[]{:S(2)}) copy-start(bf16[176,2112]{1,0:T(8,128)(2,1)} %param.27) | copy-start | bytes 2230276
  6.5 229.9 %all-gather.4.cloned.1.call-start = ((), (), s32[]{:S(2)}) async-start(), calls=%async_computation.2 | async-start | bytes 4595712 | tf_op jit(solution)/shard_map/all_gather | solution.py:462
  15.9 3.0 %copy-start = (bf16[704,528]{0,1:T(8,128)(2,1)S(1)}, bf16[704,528]{0,1:T(8,128)(2,1)}, u32[]{:S(2)}) copy-start(bf16[704,528]{0,1:T(8,128)(2,1)} %param.19) | copy-start | bytes 2230276
  18.9 1.6 copy-start.2
  18.9 2.3 copy-start.3
  19.0 2.9 %copy-start.4 = (bf16[704]{0:T(1024)(128)(2,1)S(1)}, bf16[704]{0:T(1024)(128)(2,1)}, u32[]{:S(2)}) copy-start(bf16[704]{0:T(1024)(128)(2,1)} %param.17) | copy-start | bytes 4228
  19.1 2.9 %copy-start.5 = (bf16[704]{0:T(1024)(128)(2,1)S(1)}, bf16[704]{0:T(1024)(128)(2,1)}, u32[]{:S(2)}) copy-start(bf16[704]{0:T(1024)(128)(2,1)} %param.18) | copy-start | bytes 4228
  19.1 2.9 %copy-start.13 = (bf16[176]{0:T(256)(128)(2,1)S(1)}, bf16[176]{0:T(256)(128)(2,1)}, u32[]{:S(2)}) copy-start(bf16[176]{0:T(256)(128)(2,1)} %param.26) | copy-start | bytes 1060
  19.1 2.9 %copy-start.8 = (s32[1,8]{1,0:T(1,128)S(1)}, s32[1,8]{1,0:T(1,128)}, u32[]{:S(2)}) copy-start(s32[1,8]{1,0:T(1,128)} %param.29) | copy-start | bytes 100
  19.1 2.9 %copy-start.15 = (s32[1,9]{1,0:T(1,128)S(1)}, s32[1,9]{1,0:T(1,128)}, u32[]{:S(2)}) copy-start(s32[1,9]{1,0:T(1,128)} %param.30) | copy-start | bytes 112
  19.1 3.6 %copy-start.6 = (bf16[704]{0:T(1024)(128)(2,1)S(1)}, bf16[704]{0:T(1024)(128)(2,1)}, u32[]{:S(2)}) copy-start(bf16[704]{0:T(1024)(128)(2,1)} %param.22) | copy-start | bytes 4228
  19.1 4.2 %copy-start.14 = (bf16[176]{0:T(256)(128)(2,1)S(1)}, bf16[176]{0:T(256)(128)(2,1)}, u32[]{:S(2)}) copy-start(bf16[176]{0:T(256)(128)(2,1)} %param.24) | copy-start | bytes 1060
  25.9 168.1 %copy-start.7 = (s32[4]{0:T(128)S(1)}, s32[4]{0:T(128)}, u32[]{:S(2)}) copy-start(s32[4]{0:T(128)} %param.31) | copy-start | bytes 52
  191.6 8.0 %copy-start.11 = (bf16[2,128,256]{2,1,0:T(8,128)(2,1)S(1)}, bf16[2,128,256]{2,1,0:T(8,128)(2,1)}, u32[]{:S(2)}) copy-start(bf16[2,128,256]{2,1,0:T(8,128)(2,1)} %get-tuple-element.15) | copy-start | bytes 393220
  194.8 4.9 %copy-start.9 = (bf16[2,2048,256]{2,1,0:T(8,128)(2,1)S(1)}, bf16[2,2048,256]{2,1,0:T(8,128)(2,1)}, u32[]{:S(2)}) copy-start(bf16[2,2048,256]{2,1,0:T(8,128)(2,1)} %get-tuple-element.16) | copy-start | bytes 6291460
  199.6 2.3 copy-start.10
  199.6 2.3 copy-start.12
  240.6 13.9 %all-to-all-start.1 = ((bf16[8,128,176]{1,2,0:T(8,128)(2,1)}), bf16[8,128,176]{1,2,0:T(8,128)(2,1)S(1)}, u32[]{:S(2)}, u32[]{:S(2)}) async-start(bf16[8,128,176]{1,2,0:T(8,128)(2,1)} %fusion.13), calls=%async_computation.1 | async-start | bytes 720896 | tf_op jit(solution)/shard_map/all_to_all | solution.py:532
Sparse Core Ops, SparseCore 0:
  9.6 78.7 all-gather.3

commit v4 on v3

--- a/solution.py
+++ b/solution.py
@@ -159,7 +159,7 @@
     text_col = [net.slots(cols) for _ in text_in]
     at_row, at_col = net.slots(rows), net.slots(cols)
     part_col, img_row, meta_grp = net.slots(cols), net.slots(rows), net.slots(1)
-    kv_grp, imgkv_grp = net.slots(cols), net.slots(1)
+    kv_grp, imgkv_grp = net.slots(2 * cols), net.slots(1)
     vo_grp, wd_grp = net.slots(1), net.slots(1)
 
     net.row_start(patch_ref, x_ref.at[c], x_row)
@@ -224,6 +224,7 @@
         at = (r + step) % rows
         net.arrived(wd_ref.at[at, wd_half], wd_row + at)
     net.push(wd_ref.at[:, wd_half], wd_ref.at[:, wd_half], wd_grp, grp=1 - g)
+    net.row_forward(text_ref[0].at[c], text_row[0])
     net.arrived(vo_ref.at[:, :, vo_rest], vo_grp)
     for step in range(1, hr):
         other = (mine + step) % hr
@@ -243,6 +244,7 @@
         partial += jnp.dot(quarter, proj_ref[i], preferred_element_type=F32)
     part_ref[c] = partial
     net.col_start(part_ref.at[c], part_ref.at[c], part_col)
+    net.row_forward(text_ref[1].at[c], text_row[1])
     net.col_finish(part_ref, part_col)
     image = projb_ref[...].astype(F32)
     for i in range(cols):
@@ -251,7 +253,7 @@
     net.row_start(image_ref.at[r], image_ref, img_row)
     net.row_forward(gain_ref, gain_row)
     net.row_finish(gain_ref, gain_row)
-    for b, base in zip(text_ref, text_row):
+    for b, base in zip(text_ref[2:], text_row[2:]):
         net.row_forward(b.at[c], base)
     for b, base, other in zip(text_ref, text_row, text_col):
         net.row_finish(b.at[c], base)
@@ -274,6 +276,10 @@
 
     own_rows = sum(b.shape[2] for b in text_ref[:2])
 
+    def piece_rows(at, piece):
+        first = at * own_rows + piece * (own_rows // 2)
+        return pl.ds(pl.multiple_of(first, TPD), own_rows // 2)
+
     def text_block(at):
         for piece in range(2):
             @pl.loop(0, own_rows // 2 // TPD)
@@ -292,8 +298,9 @@
                 put = pl.ds(pl.multiple_of(put, TPD), TPD)
                 q_ref[put] = found[:, :PAD]
                 kv_ref[g, put] = found[:, PAD:]
-        rows_of = pl.ds(pl.multiple_of(at * own_rows, TPD), own_rows)
-        net.push(kv_ref.at[g, rows_of], kv_ref.at[g, rows_of], kv_grp + at, grp=1 - g)
+            rows_of = piece_rows(at, piece)
+            sent = kv_ref.at[g, rows_of]
+            net.push(sent, sent, kv_grp + 2 * at + piece, grp=1 - g)
 
     text_block(c)
     net.row_finish(image_ref, img_row)
@@ -309,8 +316,8 @@
     net.arrived(imgkv_ref.at[1 - g], imgkv_grp)
     for step in range(cols):
         at = (c + step) % cols
-        rows_of = pl.ds(pl.multiple_of(at * own_rows, TPD), own_rows)
-        net.arrived(kv_ref.at[1 - g, rows_of], kv_grp + at)
+        for piece in range(2):
+            net.arrived(kv_ref.at[1 - g, piece_rows(at, piece)], kv_grp + 2 * at + piece)
     for copy in net.pending:
         copy.wait_send()
 
@@ -323,8 +330,8 @@
     tokens = count // 4
     depth = proj.shape[2]
     args = (patch, small, wv, wvb, ids[:, None], ids[None, :], vo, vob, proj, projb, gain, wd, meta) + tuple(texts)
-    sends = (6 + number) * (rows - 1) + (5 + number) * (cols - 1) + 4 + cols
-    slots = (6 + number) * rows + (5 + number) * cols + 4 + cols
+    sends = (6 + number) * (rows - 1) + (5 + number) * (cols - 1) + 4 + 2 * cols
+    slots = (6 + number) * rows + (5 + number) * cols + 4 + 2 * cols
     vmem = pl.BlockSpec(memory_space=pltpu.VMEM)
     return pl.pallas_call(
         functools.partial(

time: 264 us -> 252 us (0.955)
  Pallas kernels: 179 us -> 167 us
    pallas_call x1, Pallas kernels: 166 us -> 155 us  [front(): pl.pallas_call(functools.partial(front_kernel, texts=number, rows=rows, c...]
  transfers between devices with their start and end apart: 2 -> 2, of which waited for: 1 -> 1; matrix products, arithmetic and copies ran while one was open for 12% -> 13% of each run, Pallas kernels for 68% -> 67%
where the time goes in v4:
time: 252 us; the launch traced here: 250 us
  Pallas kernels  167 us (66%)
  local copies, waits for them, and re-layouts  19.7 us (8%)
  blocking collectives  17.9 us (7%)
  between operations  13.8 us (5%)
  matrix products  11.8 us (5%)
  waiting for transfers between devices  9.98 us (4%)
  other arithmetic  6.6 us (3%)
  starting transfers between devices  3.45 us (1%)
    pallas_call x1, Pallas kernels, front(): pl.pallas_call(functools.partial(front_kernel, texts=number, rows=rows, c...  155 us
    all_to_all x1, blocking collectives, per_device(): rows = lax.all_to_all(spread, ('col', 'row'), 0, 0)  17.9 us
    pallas_call x1, Pallas kernels, dec_attn(): pl.pallas_call(functools.partial(dec_attn_kernel, scale=scale), grid_spec...  11.8 us
    all_to_all x1, waiting for transfers between devices, per_device(): delta = lax.all_to_all(delta, 'row', 0, 0).reshape(own_text, text.shape[1])  9.27 us
    dot_general x2, matrix products, per_device(): jnp.dot(hot_half, kv_image[half], preferred_element_type=F32).astype(BF16)  5.31 us
  transfers between devices with their start and end apart: 2, of which 1 were waited for; matrix products, arithmetic and copies ran while one was open for 13% of the time, Pallas kernels for 67%

profile of v4, /device:TPU:0, one launch (start us, length us, event | category | flops | bytes accessed | tf_op | source)
XLA Modules:
  0.0 250.2 jit_solution(11953718623915422561)
XLA Ops:
  6.5 0.7 all-gather.4.cloned.1.call-update
  7.3 0.8 reduce-window.43
  8.3 0.9 tile.15.ids_ref
  9.2 0.7 tile.14.idk_ref
  9.8 0.8 dynamic_slice.15
  10.7 0.5 copy.70
  11.2 1.2 copy.56
  12.5 1.1 copy.54
  13.6 0.2 pad.57
  13.8 0.8 copy.67
  14.6 1.3 pad.58.wd_in
  15.9 1.7 copy.53
  17.6 1.3 pad.53.proj_ref
  19.1 1.4 copy.57.wv_in
  20.5 0.7 pad.52.vo_in
  21.3 0.6 copy.52
  22.1 0.6 pad.59.meta_in
  22.7 0.6 broadcast_in_dim.68.vob_ref
  23.3 0.6 broadcast_in_dim.72.projb_ref
  23.9 0.6 pad_convert_fusion.gain_in
  24.5 0.6 fusion.42.small_ref
  25.1 0.8 fusion.52
  25.9 155.1 %front.1 = (bf16[2048,128]{1,0:T(8,128)(2,1)}, bf16[2,2048,256]{2,1,0:T(8,128)(2,1)}, bf16[128,128]{1,0:T(8,128)(2,1)}, bf16[2,128,256]{2,1,0:T(8,128)(2,1)}, bf...) custom-call(bf16[64,704]{1,0:T(8,128)(2,1)} %bitcast.143, f32[8,704]{1,0:T(8,128)} %fusion.42.small_ref, ...), custom_call_target="tpu_custom_call" | custom-call | tf_op jit(solution)/shard_map/front/pallas_call | solution.py:336
  181.1 0.8 slice_bitcast_fusion
  181.9 0.2 reduce-window.45
  182.0 0.7 slice_bitcast_fusion.2
  182.7 0.2 reduce-window.46
  182.9 0.2 reduce-window.47
  183.1 0.2 reduce-window.48
  183.3 0.2 reduce-window.42
  183.8 0.4 copy.60.start_ref
  184.2 0.8 bitcast_add_fusion
  185.7 3.3 %fusion.1 = bf16[1,2048,256]{2,1,0:T(8,128)(2,1)S(1)} fusion(bf16[2,2048,256]{2,1,0:T(8,128)(2,1)} %get-tuple-element.16, pred[2048]{0:T(1024)(128)(4,1)S(1)} %fusion.33, s32[2048]{0:T(1024)S(1)} %broadcast_select_fusion.1, bf16[2,128,256]{2,1,0:T(8,128)(2,1)} %get-tuple-element.15), kind=kOutput, calls=%fused_computation.3 | convolution fusion | flops 135528448 | bytes 2172928 | tf_op jit(solution)/shard_map/dot_general | solution.py:522
  189.1 2.0 fusion.3
  191.1 0.2 fusion.18.pos_ref
  191.4 2.0 fusion.4.q_ref
  193.4 0.4 pad_maximum_fusion
  193.7 11.8 %dec_attn.1 = bf16[2048,128]{1,0:T(8,128)(2,1)S(1)} custom-call(s32[8]{0:T(128)S(1)} %and_select_fusion.low_ref, bf16[2048,128]{1,0:T(8,128)(2,1)S(1)} %fusion.4.q_ref, s32[2048,1]{1,0:T(8,128)S(1)} %copy.60.start_ref, s32[2048,1]{1,0:T(8,128)S(1)} %fusion.18.pos_ref, bf16[2,2048,128]{2,1,0:T(8,128)(2,1)S(1)} %get-tuple-element.24.k_ref, ...), custom_call_target="tpu_custom_call" | custom-call | tf_op jit(solution)/shard_map/dec_attn/pallas_call | solution.py:409
  205.6 0.2 copy.61
  205.8 17.9 %all_to_all.10 = bf16[16,128,88]{1,2,0:T(8,128)(2,1)S(1)} all-to-all(bf16[16,128,88]{1,2,0:T(8,128)(2,1)S(1)} %copy.61), channel_id=1, replica_groups=mesh['row'=8,'col'=2,'grp'=2] {'col','row'}, dimensions={0} | all-to-all | bytes 720896 | tf_op jit(solution)/shard_map/all_to_all | solution.py:533
  223.8 4.2 %fusion.13 = bf16[8,128,176]{1,2,0:T(8,128)(2,1)} fusion(bf16[2,128,704,1]{1,2,3,0:T(8,128)(2,1)S(1)} %bitcast.144, bf16[2,8,704,176]{2,3,1,0:T(8,128)(2,1)} %bitcast.154), kind=kOutput, calls=%fused_computation.24 | convolution fusion | flops 507691008 | bytes 4685824 | tf_op jit(solution)/shard_map/ctk,crkf->rtf/dot_general | solution.py:536
  227.9 3.4 %all-to-all-start.1 = ((bf16[8,128,176]{1,2,0:T(8,128)(2,1)}), bf16[8,128,176]{1,2,0:T(8,128)(2,1)S(1)}, u32[]{:S(2)}, u32[]{:S(2)}) async-start(bf16[8,128,176]{1,2,0:T(8,128)(2,1)} %fusion.13), calls=%async_computation.1 | async-start | bytes 720896 | tf_op jit(solution)/shard_map/all_to_all | solution.py:539
  231.4 0.9 dynamic-slice_bitcast_fusion
  232.3 0.3 iota_compare_fusion.2
  232.6 9.3 %all-to-all-done.1 = bf16[8,128,176]{1,2,0:T(8,128)(2,1)S(1)} async-done(((bf16[8,128,176]{1,2,0:T(8,128)(2,1)}), bf16[8,128,176]{1,2,0:T(8,128)(2,1)S(1)}, u32[]{:S(2)}, u32[]{:S(2)}) %all-to-all-start.1) | async-done | bytes 360480 | tf_op jit(solution)/shard_map/all_to_all | solution.py:539
  241.9 0.2 copy.63
  242.1 0.3 fusion.12
  242.4 0.9 copy.64
  (64 shorter events, 1.7 us)
Async XLA Ops:
  6.5 5.9 %copy-start.1 = (bf16[176,2112]{1,0:T(8,128)(2,1)S(1)}, bf16[176,2112]{1,0:T(8,128)(2,1)}, u32[]{:S(2)}) copy-start(bf16[176,2112]{1,0:T(8,128)(2,1)} %param.27) | copy-start | bytes 2230276
  6.5 217.2 %all-gather.4.cloned.1.call-start = ((), (), s32[]{:S(2)}) async-start(), calls=%async_computation.2 | async-start | bytes 4595712 | tf_op jit(solution)/shard_map/all_gather | solution.py:469
  15.9 3.0 %copy-start = (bf16[704,528]{0,1:T(8,128)(2,1)S(1)}, bf16[704,528]{0,1:T(8,128)(2,1)}, u32[]{:S(2)}) copy-start(bf16[704,528]{0,1:T(8,128)(2,1)} %param.19) | copy-start | bytes 2230276
  18.9 1.6 copy-start.2
  18.9 2.3 copy-start.3
  19.0 2.9 %copy-start.4 = (bf16[704]{0:T(1024)(128)(2,1)S(1)}, bf16[704]{0:T(1024)(128)(2,1)}, u32[]{:S(2)}) copy-start(bf16[704]{0:T(1024)(128)(2,1)} %param.17) | copy-start | bytes 4228
  19.1 2.9 %copy-start.5 = (bf16[704]{0:T(1024)(128)(2,1)S(1)}, bf16[704]{0:T(1024)(128)(2,1)}, u32[]{:S(2)}) copy-start(bf16[704]{0:T(1024)(128)(2,1)} %param.18) | copy-start | bytes 4228
  19.1 2.9 %copy-start.13 = (bf16[176]{0:T(256)(128)(2,1)S(1)}, bf16[176]{0:T(256)(128)(2,1)}, u32[]{:S(2)}) copy-start(bf16[176]{0:T(256)(128)(2,1)} %param.26) | copy-start | bytes 1060
  19.1 2.9 %copy-start.8 = (s32[1,8]{1,0:T(1,128)S(1)}, s32[1,8]{1,0:T(1,128)}, u32[]{:S(2)}) copy-start(s32[1,8]{1,0:T(1,128)} %param.29) | copy-start | bytes 100
  19.1 2.9 %copy-start.15 = (s32[1,9]{1,0:T(1,128)S(1)}, s32[1,9]{1,0:T(1,128)}, u32[]{:S(2)}) copy-start(s32[1,9]{1,0:T(1,128)} %param.30) | copy-start | bytes 112
  19.1 3.6 %copy-start.6 = (bf16[704]{0:T(1024)(128)(2,1)S(1)}, bf16[704]{0:T(1024)(128)(2,1)}, u32[]{:S(2)}) copy-start(bf16[704]{0:T(1024)(128)(2,1)} %param.22) | copy-start | bytes 4228
  19.1 4.2 %copy-start.14 = (bf16[176]{0:T(256)(128)(2,1)S(1)}, bf16[176]{0:T(256)(128)(2,1)}, u32[]{:S(2)}) copy-start(bf16[176]{0:T(256)(128)(2,1)} %param.24) | copy-start | bytes 1060
  25.9 157.5 %copy-start.7 = (s32[4]{0:T(128)S(1)}, s32[4]{0:T(128)}, u32[]{:S(2)}) copy-start(s32[4]{0:T(128)} %param.31) | copy-start | bytes 52
  181.0 8.0 %copy-start.11 = (bf16[2,128,256]{2,1,0:T(8,128)(2,1)S(1)}, bf16[2,128,256]{2,1,0:T(8,128)(2,1)}, u32[]{:S(2)}) copy-start(bf16[2,128,256]{2,1,0:T(8,128)(2,1)} %get-tuple-element.15) | copy-start | bytes 393220
  184.2 4.9 %copy-start.9 = (bf16[2,2048,256]{2,1,0:T(8,128)(2,1)S(1)}, bf16[2,2048,256]{2,1,0:T(8,128)(2,1)}, u32[]{:S(2)}) copy-start(bf16[2,2048,256]{2,1,0:T(8,128)(2,1)} %get-tuple-element.16) | copy-start | bytes 6291460
  189.0 2.3 copy-start.10
  189.0 2.3 copy-start.12
  227.9 13.9 %all-to-all-start.1 = ((bf16[8,128,176]{1,2,0:T(8,128)(2,1)}), bf16[8,128,176]{1,2,0:T(8,128)(2,1)S(1)}, u32[]{:S(2)}, u32[]{:S(2)}) async-start(bf16[8,128,176]{1,2,0:T(8,128)(2,1)} %fusion.13), calls=%async_computation.1 | async-start | bytes 720896 | tf_op jit(solution)/shard_map/all_to_all | solution.py:539
Sparse Core Ops, SparseCore 0:
  9.6 78.7 all-gather.3
